TPU v7x, 256 devices: a whole 4x4x8 slice. The times are simulated.
256 devices in a mesh: row: 16 (over y, x), col: 8 (over z), rep: 2 (over core).
Axes of the slice: x: 4, y: 4, z: 8, core: 2. Of those that a mesh axis runs over, the one named last changes fastest.
Arguments:
- features: float32 [32768, 128], P(('row', 'col')), may hold values from -6 to 6
- cotangent: float32 [32768, 256], P(('row', 'col')), may hold values from -6 to 6
- w_self: float32 [128, 256], replicated, may hold values from -0.5 to 0.5
- w_neigh: float32 [128, 256], replicated, may hold values from -1.5 to 1.5
- bias: float32 [256], replicated, may hold values from -3 to 3
- tiles: float32 [16, 8, 184, 128, 128], P('row', 'col'), may hold values from 0 to 2.1, as said below
- tile_dst: int32 [16, 8, 184], P('row', 'col'), may hold values from 0 to 31
- tile_src: int32 [16, 8, 184], P('row', 'col'), may hold values from 0 to 15
- tile_count: int32 [16, 8], P('row', 'col'), may hold values from 61 to 184, as said below
Outputs:
- hidden: float32 [32768, 256], P(('row', 'col'), 'rep')
- grad_features: float32 [32768, 128], P(('row', 'col'), 'rep')
- grad_self: float32 [128, 256], P(None, 'rep')
- grad_neigh: float32 [128, 256], P(None, 'rep')
- grad_bias: float32 [256], P('rep')
Inputs may be any that keep to these rules, and one draw needn't show every extreme that they name: `tiles`: entries are 0 (no edge) or an edge weight. Slots at positions tile_count and beyond are ignored; some cell has all 184 slots live.
All inputs are finite; a program needn't handle non-finite values.
Results may differ from a plain program's by a relative error of at most 0.0003.
Values sent between devices are 32-bit elements; how exact they have to be, the bound alone decides.
A program may use at most 128 MiB of HBM per device.

v0:
```python
import jax
import jax.numpy as jnp
from jax import lax
from jax.sharding import PartitionSpec as P


def shards(features, cotangent, w_self, w_neigh, bias, tiles, tile_dst, tile_src, tile_count):
    highest = lax.Precision.HIGHEST
    weights = tiles[0, 0]
    dst_index = tile_dst[0, 0]
    src_index = tile_src[0, 0]
    slot_count = weights.shape[0]
    block_size = weights.shape[1]
    node_rows = features.shape[0]
    block_count = node_rows // block_size
    feat_width = features.shape[1]
    half_width = feat_width // 2
    hid_half = w_self.shape[1] // 2
    row_count = lax.axis_size("row")
    col_count = lax.axis_size("col")
    rep_index = lax.axis_index("rep")
    live_mask = (jnp.arange(slot_count, dtype=jnp.int32) < tile_count[0, 0]).astype(jnp.float32)
    dst_onehot = (
        dst_index[None, :] == jnp.arange(row_count * block_count, dtype=jnp.int32)[:, None]
    ).astype(jnp.float32)
    src_onehot = (
        src_index[None, :] == jnp.arange(col_count * block_count, dtype=jnp.int32)[:, None]
    ).astype(jnp.float32)
    width = features.shape[1]
    gathered = lax.all_gather(features, "col", axis=0, tiled=True)
    source_blocks = gathered.reshape(col_count * block_count, block_size, width)[src_index]
    products = (
        jnp.einsum("tab,tbf->taf", weights, source_blocks, precision=highest)
        * live_mask[:, None, None]
    )
    partial_value = jnp.einsum(
        "st,tx->sx", dst_onehot, products.reshape(slot_count, block_size * width), precision=highest
    )
    partial_value = partial_value.reshape(row_count * node_rows, width)
    row_weight = jnp.sum(weights, axis=2) * live_mask[:, None]
    degree_part = jnp.einsum("st,tx->sx", dst_onehot, row_weight, precision=highest).reshape(
        row_count * node_rows
    )
    summed, degree = (
        lax.psum_scatter(partial_value, "row", scatter_dimension=0, tiled=True),
        lax.psum_scatter(degree_part, "row", scatter_dimension=0, tiled=True),
    )
    inverse = 1.0 / jnp.maximum(degree, 1.0)
    aggregate_part = summed * inverse[:, None]
    preact = jnp.dot(features, w_self, precision=highest, preferred_element_type=jnp.float32)
    preact = (
        preact
        + jnp.dot(aggregate_part, w_neigh, precision=highest, preferred_element_type=jnp.float32)
        + bias
    )
    gating = jax.nn.sigmoid(preact)
    hidden = preact * gating
    grad_pre = cotangent * (gating * (1.0 + preact * (1.0 - gating)))
    grad_half = lax.dynamic_slice_in_dim(grad_pre, rep_index * hid_half, hid_half, 1)
    self_term = jnp.einsum("nf,nh->fh", features, grad_half, precision=highest)
    neigh_term = jnp.einsum("nf,nh->fh", aggregate_part, grad_half, precision=highest)
    bias_term = jnp.sum(grad_half, axis=0)
    grad_self, grad_neigh, grad_bias = lax.psum((self_term, neigh_term, bias_term), ("row", "col"))
    factor = float(node_rows * row_count * col_count) ** (-0.5)
    scaled = jnp.einsum("nh,fh->nf", grad_pre, w_neigh, precision=highest) * inverse[:, None]
    dest_values = lax.all_gather(scaled, "row", axis=0, tiled=True)
    dest_blocks = dest_values.reshape(row_count * block_count, block_size, width)[dst_index]
    back_products = (
        jnp.einsum("tab,taf->tbf", weights, dest_blocks, precision=highest)
        * live_mask[:, None, None]
    )
    source_part = jnp.einsum(
        "st,tx->sx",
        src_onehot,
        back_products.reshape(slot_count, block_size * width),
        precision=highest,
    )
    source_part = source_part.reshape(col_count * node_rows, width)
    back = lax.psum_scatter(source_part, "col", scatter_dimension=0, tiled=True)
    direct = jnp.einsum("nh,fh->nf", grad_pre, w_self, precision=highest)
    grad_features = lax.dynamic_slice_in_dim(direct + back, rep_index * half_width, half_width, 1)
    hidden_half = lax.dynamic_slice_in_dim(hidden, rep_index * hid_half, hid_half, 1)
    return (hidden_half, grad_features, grad_self * factor, grad_neigh * factor, grad_bias * factor)


def solution(mesh):
    return jax.shard_map(
        shards,
        mesh=mesh,
        in_specs=(
            P(("row", "col"), None),
            P(("row", "col"), None),
            P(),
            P(),
            P(),
            P("row", "col", None, None, None),
            P("row", "col", None),
            P("row", "col", None),
            P("row", "col"),
        ),
        out_specs=(
            P(("row", "col"), "rep"),
            P(("row", "col"), "rep"),
            P(None, "rep"),
            P(None, "rep"),
            P("rep"),
        ),
        check_vma=False,
    )
```

profile of v0, /device:TPU:0, one launch (start us, length us, event | category | flops | bytes accessed | tf_op | source)
XLA Modules:
  0.0 675.6 jit_solution(14046572293660637089)
XLA Ops:
  7.2 0.7 all-gather.3.cloned.1.call-update
  8.6 0.7 compare_select_fusion.1
  9.3 40.5 %all-gather.3.cloned.1.call-done = f32[2048,128]{1,0:T(8,128)} async-done(((f32[256,128]{1,0:T(8,128)}), f32[2048,128]{1,0:T(8,128)}) %all-gather.3.cloned.1.call-update) | async-done | bytes 1048592 | tf_op jit(solution)/shard_map/all_gather | solution.py:30
  49.8 11.8 %gather_fusion = f32[184,128,128]{2,1,0:T(8,128)} fusion(f32[16,128,128]{2,1,0:T(8,128)} %bitcast.48, s32[1024]{0:T(1024)S(1)} %pad_clamp_fusion.1), kind=kCustom, calls=%fused_computation | custom fusion | bytes 24117984 | tf_op jit(solution)/shard_map/gather | solution.py:31
  61.6 26.7 %multiply_bitcast_fusion.1 = f32[184,128,128]{1,2,0:T(8,128)} fusion(f32[184]{0:T(256)S(1)} %compare_convert_fusion, f32[184,128,128]{2,1,0:T(8,128)} %gather_fusion, f32[1,1,184,128,128]{4,3,2,1,0:T(8,128)} %param.14), kind=kOutput, calls=%fused_computation.13 | convolution fusion | flops 4633526272 | bytes 36176608 | tf_op jit(solution)/shard_map/tab,tbf->taf/dot_general | solution.py:33
  88.2 12.3 %copy.26 = f32[184,128,128]{2,1,0:T(8,128)} copy(f32[184,128,128]{1,2,0:T(8,128)} %multiply_bitcast_fusion.1) | data formatting | bytes 24117248 | tf_op jit(solution)/shard_map/mul | solution.py:33
  100.6 15.7 %fusion.3 = f32[32,16384]{1,0:T(8,128)S(1)} fusion(f32[23,8,128,128]{3,2,1,0:T(8,128)} %bitcast.50, s32[184]{0:T(256)S(1)} %bitcast.52), kind=kOutput, calls=%fused_computation.5 | convolution fusion | flops 1157633792 | bytes 14156512 | tf_op jit(solution)/shard_map/st,tx->sx/dot_general | solution.py:36
  116.3 1.5 reshape.103
  118.0 0.6 dynamic-slice
  119.2 7.6 %reduce_sum.18 = f32[184,128]{1,0:T(8,128)S(1)} reduce(f32[1,1,184,128,128]{4,3,2,1,0:T(8,128)} %param.14, f32[]{:T(128)} %constant.13.clone.1), dimensions={0,1,4}, to_apply=%region_1.0 | reduce | flops 2991104 | bytes 12152836 | tf_op jit(solution)/shard_map/reduce_sum | solution.py:40
  126.8 0.2 convolution_bitcast_fusion.1
  127.0 74.3 %all-reduce = f32[4096]{0:T(1024)S(1)} all-reduce(f32[4096]{0:T(1024)S(1)} %convolution_bitcast_fusion.1), channel_id=3, replica_groups=mesh['row'=16,'col'=8,'rep'=2] {'row'}, use_global_device_ids=true, to_apply=%region_2.0.clone | all-reduce | flops 4096 | bytes 32768
  201.4 0.4 fusion.30
  201.9 1.4 multiply_multiply_fusion
  203.3 1.0 convolution_multiply_fusion
  204.4 1.0 convolution_bitcast_fusion
  205.4 2.0 fusion.15
  207.5 41.1 %all-gather.5.cloned.1.call-done = f32[4096,128]{1,0:T(8,128)} async-done(((f32[256,128]{1,0:T(8,128)}), f32[4096,128]{1,0:T(8,128)}) %all-gather.5.cloned.1.call-update) | async-done | bytes 2097168 | tf_op jit(solution)/shard_map/all_gather | solution.py:66
  248.5 12.4 %gather_fusion.1 = f32[184,128,128]{2,1,0:T(8,128)} fusion(f32[32,128,128]{2,1,0:T(8,128)} %bitcast.49, s32[1024]{0:T(1024)S(1)} %pad_clamp_fusion), kind=kCustom, calls=%fused_computation.1 | custom fusion | bytes 24117984 | tf_op jit(solution)/shard_map/gather | solution.py:67
  260.9 26.1 %multiply_bitcast_fusion = f32[184,128,128]{1,2,0:T(8,128)} fusion(f32[184]{0:T(256)S(1)} %compare_convert_fusion, f32[184,128,128]{2,1,0:T(8,128)} %gather_fusion.1, f32[1,1,184,128,128]{4,3,2,1,0:T(8,128)} %param.14), kind=kOutput, calls=%fused_computation.12 | convolution fusion | flops 4633526272 | bytes 36176608 | tf_op jit(solution)/shard_map/tab,taf->tbf/dot_general | solution.py:69
  287.0 12.4 %copy.28 = f32[184,128,128]{2,1,0:T(8,128)} copy(f32[184,128,128]{1,2,0:T(8,128)} %multiply_bitcast_fusion) | data formatting | bytes 24117248 | tf_op jit(solution)/shard_map/mul | solution.py:69
  299.3 14.8 %fusion = f32[16,16384]{1,0:T(8,128)S(1)} fusion(f32[23,8,128,128]{3,2,1,0:T(8,128)} %bitcast.51, s32[184]{0:T(256)S(1)} %bitcast.56), kind=kOutput, calls=%fused_computation.2 | convolution fusion | flops 578816896 | bytes 13107936 | tf_op jit(solution)/shard_map/st,tx->sx/dot_general | solution.py:72
  314.2 0.2 reshape.107
  314.4 1.3 copy.29
  315.7 347.6 %psum.23 = f32[128]{0:T(128)S(1)} all-reduce(f32[128]{0:T(128)S(1)} %dynamic-slice_reduce_fusion), channel_id=1, replica_groups=mesh['row'=16,'col'=8,'rep'=2] {'row','col'}, use_global_device_ids=true, to_apply=%region_7.0 | all-reduce | flops 128 | bytes 1024 | tf_op jit(solution)/shard_map/psum | solution.py:63
  663.4 0.7 dynamic-slice_multiply_fusion
  664.1 0.5 broadcast_multiply_fusion.2
  664.6 0.4 fusion.31
  665.0 0.9 broadcast_multiply_fusion
  665.9 0.7 copy.32
  666.6 0.7 copy.31
  667.3 1.5 dynamic-slice_add_fusion
  (36 shorter events, 0.5 us)
Async XLA Ops:
  7.2 194.7 %copy-start = (f32[128,256]{1,0:T(8,128)S(1)}, f32[128,256]{1,0:T(8,128)}, u32[]{:S(2)}) copy-start(f32[128,256]{1,0:T(8,128)} %param.12) | copy-start | bytes 393220
  7.2 42.6 %all-gather.3.cloned.1.call-start = ((), (), s32[]{:S(2)}) async-start(), calls=%async_computation.2 | async-start | bytes 1179648 | tf_op jit(solution)/shard_map/all_gather | solution.py:30
  7.9 193.9 %reduce-scatter.3.cloned.1.call-start = ((), (), s32[]{:S(2)}) async-start(), calls=%async_computation.3 | async-start | bytes 2228224 | tf_op jit(solution)/shard_map/reduce_scatter | solution.py:45
  88.2 12.3 %copy-start.5 = (s32[1,1,184]{2,1,0:T(1,128)S(1)}, s32[1,1,184]{2,1,0:T(1,128)}, u32[]{:S(2)}) copy-start(s32[1,1,184]{2,1,0:T(1,128)} %param.15) | copy-start | bytes 2212
  100.5 17.4 %copy-start.8 = (u32[256]{0:T(256)S(1)}, u32[256]{0:T(256)}, u32[]{:S(2)}) copy-start(u32[256]{0:T(256)} %constant.31) | copy-start | bytes 3076
  116.3 85.1 %copy-start.2 = (f32[256,128]{1,0:T(8,128)S(1)}, f32[256,128]{1,0:T(8,128)}, u32[]{:S(2)}) copy-start(f32[256,128]{1,0:T(8,128)} %param.9) | copy-start | bytes 393220
  116.3 85.1 %copy-start.3 = (f32[128,256]{1,0:T(8,128)S(1)}, f32[128,256]{1,0:T(8,128)}, u32[]{:S(2)}) copy-start(f32[128,256]{1,0:T(8,128)} %param.11) | copy-start | bytes 393220
  116.3 85.5 %copy-start.4 = (f32[256,256]{1,0:T(8,128)S(1)}, f32[256,256]{1,0:T(8,128)}, u32[]{:S(2)}) copy-start(f32[256,256]{1,0:T(8,128)} %param.10) | copy-start | bytes 786436
  116.3 85.5 %copy-start.7 = (f32[256]{0:T(256)S(1)}, f32[256]{0:T(256)}, u32[]{:S(2)}) copy-start(f32[256]{0:T(256)} %param.13) | copy-start | bytes 3076
  117.9 130.7 %all-gather.5.cloned.1.call-start = ((), (), s32[]{:S(2)}) async-start(), calls=%async_computation.4 | async-start | bytes 2228224 | tf_op jit(solution)/shard_map/all_gather | solution.py:66
  204.3 460.7 %all-reduce.4.cloned.1.call-start = ((), (), s32[]{:S(2)}) async-start(), calls=%async_computation.6 | async-start | bytes 262144 | tf_op jit(solution)/shard_map/psum | solution.py:63
  207.4 459.9 %reduce-scatter.5.cloned.1.call-start = ((), (), s32[]{:S(2)}) async-start(), calls=%async_computation.5 | async-start | bytes 1179648 | tf_op jit(solution)/shard_map/reduce_scatter | solution.py:79
  287.0 12.4 %copy-start.6 = (s32[1,1,184]{2,1,0:T(1,128)S(1)}, s32[1,1,184]{2,1,0:T(1,128)}, u32[]{:S(2)}) copy-start(s32[1,1,184]{2,1,0:T(1,128)} %param.16) | copy-start | bytes 2212
  287.0 381.9 %copy-start.1 = (f32[128,256]{1,0:T(8,128)S(1)}, f32[128,256]{1,0:T(8,128)}, u32[]{:S(2)}) copy-start(f32[128,256]{1,0:T(8,128)} %param.12) | copy-start | bytes 393220
Sparse Core Ops, SparseCore 0:
  9.8 39.9 all-gather.2
  118.0 77.8 reduce-scatter.2
  204.4 44.0 all-gather.4
  255.5 211.3 all-reduce.3
  469.3 36.2 reduce-scatter.4
where the time goes:
time: 684 us; the launch traced here: 676 us
  blocking collectives  422 us (62%)
  matrix products  89.7 us (13%)
  waiting for transfers between devices  82.3 us (12%)
  local copies, waits for them, and re-layouts  53.9 us (8%)
  between operations  15.5 us (2%)
  other arithmetic  12 us (2%)
    psum x1, blocking collectives, shards(): lax.psum((self_term, neigh_term, bias_term), ('row', 'col'))  348 us
    unnamed x1, blocking collectives  74.3 us
    all_gather x1, waiting for transfers between devices, shards(): dest_values = lax.all_gather(scaled, 'row', axis=0, tiled=True)  41.1 us
    all_gather x1, waiting for transfers between devices, shards(): gathered = lax.all_gather(features, 'col', axis=0, tiled=True)  40.5 us
    dot_general x1, matrix products, shards(): jnp.einsum('tab,tbf->taf', weights, source_blocks, precision=highest)  26.7 us
    dot_general x1, matrix products, shards(): jnp.einsum('tab,taf->tbf', weights, dest_blocks, precision=highest)  26.1 us
    dot_general x1, matrix products, shards(): jnp.einsum('st,tx->sx', dst_onehot, products.reshape(slot_count, block_si...  15.7 us
    dot_general x1, matrix products, shards(): jnp.einsum('st,tx->sx', src_onehot, back_products.reshape(slot_count, blo...  14.8 us
  transfers between devices with their start and end apart: 5, of which 2 were waited for; matrix products, arithmetic and copies ran while one was open for 12% of the time, Pallas kernels for 0%

commit v1 on v0

v1 whole, which is shorter than its diff:
```python
import functools

import jax
import jax.numpy as jnp
from jax import lax
from jax.experimental import pallas as pl
from jax.experimental.pallas import tpu as pltpu
from jax.sharding import PartitionSpec as P

MESH = pl.DeviceIdType.MESH
F32 = jnp.float32
BF16 = jnp.bfloat16
VMEM = pltpu.VMEM
DMA = pltpu.SemaphoreType.DMA
MIB = 1 << 20


def split(value):
    high = value.astype(BF16)
    low = (value - high.astype(F32)).astype(BF16)
    return high, low


def dot3(left, right, dims=((1,), (0,))):
    left_high, left_low = split(left)
    right_high, right_low = split(right)

    def one(a, b):
        return lax.dot_general(a, b, (dims, ((), ())), preferred_element_type=F32)

    return one(left_high, right_high) + (one(left_high, right_low) + one(left_low, right_high))


def remote(src, dst, send, recv, **where):
    return pltpu.make_async_remote_copy(
        src_ref=src, dst_ref=dst, send_sem=send, recv_sem=recv, device_id=where, device_id_type=MESH
    )


def greet(partners):
    barrier = pltpu.get_barrier_semaphore()
    for where in partners:
        pl.semaphore_signal(barrier, inc=1, device_id=where, device_id_type=MESH)
    pl.semaphore_wait(barrier, len(partners))


def gather_kernel(cols, feat, stacked, held, ring_send, ring_recv, pair_send, pair_recv):
    z = lax.axis_index("col")
    rep = lax.axis_index("rep")
    other = 1 - rep
    half = feat.shape[1] // 2
    steps = cols // 2
    step_of = {0: 1, 1: -1}
    greet(({"col": (z + 1) % cols}, {"col": (z + cols - 1) % cols}, {"rep": other}))

    def put(block, value):
        high, low = split(value)
        width = value.shape[1]
        stacked[block, :width, :width] = high
        stacked[block, :width, width:] = low
        stacked[block, width:, :width] = high
        stacked[block, width:, width:] = jnp.zeros_like(high)

    def rows(chunk):
        return pl.ds(chunk * half, half)

    def ring(way, step, chunk):
        origin = (z - step_of[way] * (step - 1) + cols) % cols
        dst = held.at[origin, rep, rows(chunk)]
        src = feat.at[rep, rows(chunk)] if step == 1 else dst
        return remote(
            src, dst, ring_send.at[way, step - 1, chunk], ring_recv.at[way, step - 1, chunk],
            col=(z + step_of[way] + cols) % cols,
        )

    def arrival(way, step, chunk):
        origin = (z - step_of[way] * step + cols) % cols
        dst = held.at[origin, rep, rows(chunk)]
        return remote(
            dst, dst, ring_send.at[way, step - 1, chunk], ring_recv.at[way, step - 1, chunk],
            col=(z + step_of[way] + cols) % cols,
        )

    def pair(way, step, chunk, core):
        origin = (z - step_of[way] * step + cols) % cols
        dst = held.at[origin, core, rows(chunk)]
        return remote(
            dst, dst, pair_send.at[way, step - 1, chunk], pair_recv.at[way, step - 1, chunk], rep=other
        )

    def messages(step):
        if step < steps:
            return [(way, chunk) for chunk in (0, 1) for way in (0, 1)]
        return [(0, 0), (1, 1)]

    for step in range(1, steps + 1):
        for way, chunk in messages(step):
            if step > 1:
                arrival(way, step - 1, chunk).wait_recv()
            ring(way, step, chunk).start()
            if step > 1:
                pair(way, step - 1, chunk, rep).start()
        if step > 1:
            for way, chunk in messages(step - 1):
                if (way, chunk) not in messages(step):
                    arrival(way, step - 1, chunk).wait_recv()
                    pair(way, step - 1, chunk, rep).start()
        if step == 1:
            for core in (0, 1):
                put(z * 2 + core, feat[core])
        else:
            for way in (0, 1):
                origin = (z - step_of[way] * (step - 1) + cols) % cols
                put(origin * 2 + rep, held[origin, rep])
    for way, chunk in messages(steps):
        arrival(way, steps, chunk).wait_recv()
        pair(way, steps, chunk, rep).start()
    far = (z + steps) % cols
    put(far * 2 + rep, held[far, rep])
    for step in range(1, steps + 1):
        for way, chunk in messages(step):
            pair(way, step, chunk, other).wait_recv()
        for way in (0, 1) if step < steps else (0,):
            origin = (z - step_of[way] * step + cols) % cols
            put(origin * 2 + other, held[origin, other])
    for step in range(1, steps + 1):
        for way, chunk in messages(step):
            ring(way, step, chunk).wait_send()
            pair(way, step, chunk, rep).wait_send()


def gather_features(feat, cols):
    block, width = feat.shape[1:]
    sems = (2, cols // 2, 2)
    return pl.pallas_call(
        functools.partial(gather_kernel, cols),
        out_shape=jax.ShapeDtypeStruct((cols * 2, 2 * width, 2 * width), BF16),
        in_specs=[pl.BlockSpec(memory_space=VMEM)],
        out_specs=pl.BlockSpec(memory_space=VMEM),
        scratch_shapes=[VMEM((cols, 2, block, width), F32), DMA(sems), DMA(sems), DMA(sems), DMA(sems)],
        compiler_params=pltpu.CompilerParams(
            collective_id=0, has_side_effects=True, vmem_limit_bytes=32 * MIB
        ),
        name="gather_features",
    )(feat)


UNROLL = 4


def fetch_own(count, dst, src, tiles, held, dst_list, src_list, sems, dummy):
    rep = lax.axis_index("rep")

    def copy(slot, place):
        return pltpu.make_async_copy(tiles.at[slot], held.at[place], sems.at[place])

    def look(slot, place):
        block = dst[0, 0, slot]
        own = (block & 1) == rep

        @pl.when(own)
        def _():
            copy(slot, place).start()
            dst_list[place] = block >> 1
            src_list[place] = src[0, 0, slot]

        return place + own.astype(jnp.int32)

    total = lax.fori_loop(0, count[0, 0], look, 0)
    groups = (total + (UNROLL - 1)) // UNROLL

    def pad(place, carry):
        copy(0, place).start()
        dst_list[place] = dummy[0]
        src_list[place] = dummy[1]
        return carry

    lax.fori_loop(total, groups * UNROLL, pad, 0)
    return groups, copy


def forward_kernel(count, dst, src, tiles, stacked, sums, held, weight, dst_list, src_list, sems):
    block = held.shape[1]
    live = sums.shape[0] - 1
    groups, copy = fetch_own(count, dst, src, tiles, held, dst_list, src_list, sems, (4 * live, 0))
    sums[...] = jnp.zeros_like(sums)
    weight[...] = jnp.zeros_like(weight)

    def step(group, carry):
        for u in range(UNROLL):
            copy(0, group * UNROLL + u).wait()
        parts = []
        for u in range(UNROLL):
            place = group * UNROLL + u
            tile = held[place]
            high, low = split(tile)
            product = jnp.dot(
                jnp.concatenate([high, low], axis=1), stacked[src_list[place]], preferred_element_type=F32
            )
            target = dst_list[place]
            parts.append((target, product[:, :block] + product[:, block:], tile))
        for target, value, tile in parts:
            sums[target >> 2, target & 3, pl.ds(8, block)] += value
            weight[target] += tile
        return carry

    lax.fori_loop(0, groups, step, 0)
    ones = jnp.ones((8, block), F32)

    def degree(target, carry):
        sums[target >> 2, target & 3, pl.ds(0, 8)] = lax.dot_general(
            ones, weight[target], (((1,), (1,)), ((), ())),
            precision=lax.Precision.HIGHEST, preferred_element_type=F32,
        )
        return carry

    lax.fori_loop(0, 4 * live, degree, 0)


def backward_kernel(count, dst, src, tiles, stacked, sums, held, dst_list, src_list, sems):
    block = held.shape[1]
    live = sums.shape[0] - 1
    groups, copy = fetch_own(count, dst, src, tiles, held, dst_list, src_list, sems, (0, live))
    sums[...] = jnp.zeros_like(sums)

    def step(group, carry):
        for u in range(UNROLL):
            copy(0, group * UNROLL + u).wait()
        parts = []
        for u in range(UNROLL):
            place = group * UNROLL + u
            high, low = split(held[place])
            right = jnp.concatenate(
                [
                    jnp.concatenate([high, low], axis=1),
                    jnp.concatenate([high, jnp.zeros_like(high)], axis=1),
                ],
                axis=0,
            )
            product = jnp.dot(stacked[dst_list[place]], right, preferred_element_type=F32)
            parts.append((src_list[place], product[:, :block] + product[:, block:]))
        for target, value in parts:
            sums[target] += value
        return carry

    lax.fori_loop(0, groups, step, 0)


def tile_call(kernel, name, out_shape, scratch, count, dst, src, tiles, stacked):
    slots, block = tiles.shape[:2]
    padded = slots + UNROLL
    smem = pl.BlockSpec(memory_space=pltpu.SMEM)
    vmem = pl.BlockSpec(memory_space=VMEM)
    return pl.pallas_call(
        kernel,
        out_shape=jax.ShapeDtypeStruct(out_shape, F32),
        in_specs=[smem, smem, smem, pl.BlockSpec(memory_space=pl.ANY), vmem],
        out_specs=vmem,
        scratch_shapes=[VMEM((padded, block, block), F32)]
        + scratch
        + [pltpu.SMEM((padded,), jnp.int32), pltpu.SMEM((padded,), jnp.int32), DMA((padded,))],
        compiler_params=pltpu.CompilerParams(vmem_limit_bytes=40 * MIB),
        name=name,
    )(count, dst, src, tiles, stacked)


SIDE = 4
DEG = 8


def middle_kernel(
    sums, feat, cot, w_self, w_neigh, bias,
    hidden_out, stacked, direct_out, grad_part,
    far1, near1, part1, far2, near2, gathered, hidden_half, hidden_got, direct_half, direct_got,
    grads, grads_got, grads_rows,
    rs_send, rs_recv, ag_send, ag_recv, pair_send, pair_recv, row_send, row_recv,
):
    row = lax.axis_index("row")
    rep = lax.axis_index("rep")
    other = 1 - rep
    rows = SIDE * SIDE
    block = feat.shape[1]
    width = feat.shape[2]
    hid = w_self.shape[1] // 2
    coords = (row % SIDE, row // SIDE)
    peers = [(row + off) % rows for off in range(1, rows)]
    greet([{"row": peer} for peer in peers] + [{"rep": other}])

    def index(axis, first, second):
        return (second, first) if axis == 0 else (first, second)

    def neighbour(axis, way):
        here = (coords[axis] + way + SIDE) % SIDE
        rest = coords[1 - axis]
        y, x = (rest, here) if axis == 0 else (here, rest)
        return y * SIDE + x

    low = block // 2
    spans = ((0, DEG + low), (DEG + low, low))
    cuts = (40, 32)
    ways = (1, -1)

    def line(axis, first, seconds):
        lo, n = spans[axis]
        start, size = seconds
        where = pl.ds(start, size)
        if axis == 0:
            return sums.at[where, first, pl.ds(lo, n)]
        return sums.at[first, where, pl.ds(lo, n)]

    def rs(axis, kind, way):
        first, second = coords[axis], coords[1 - axis]
        n = spans[axis][1]
        w = ways[way]
        mine = (0, 2) if way == 0 else (2, 2)
        rest = (2, 2) if way == 0 else (0, 2)
        sems = (rs_send.at[axis, kind, way], rs_recv.at[axis, kind, way])
        if kind < 3:
            to = neighbour(axis, w)
            if kind == 0:
                src = line(axis, (first + 2) % SIDE, mine)
                dst = far1.at[axis, way, :, pl.ds(0, n)]
            elif kind == 1:
                src = line(axis, (first + w + SIDE) % SIDE, rest)
                dst = near1.at[axis, way, pl.ds(rest[0], 2), pl.ds(0, n)]
            else:
                src = far1.at[axis, way, :, pl.ds(0, n)]
                dst = near1.at[axis, way, pl.ds(mine[0], 2), pl.ds(0, n)]
        else:
            to = neighbour(1 - axis, w)
            cut = cuts[axis]
            if kind == 3:
                lo, size = (0, cut) if way == 0 else (cut, n - cut)
                src = part1.at[axis, (second + 2) % SIDE, pl.ds(lo, size)]
                dst = far2.at[axis, way, pl.ds(0, size)]
            else:
                src = part1.at[axis, (second + w + SIDE) % SIDE, pl.ds(0, n)]
                dst = near2.at[axis, way, pl.ds(0, n)]
        return remote(src, dst, *sems, row=to)

    both = [(axis, way) for axis in (0, 1) for way in (0, 1)]
    for kind in (0, 1):
        for axis, way in both:
            rs(axis, kind, way).start()
    own_feat = feat[rep]
    pre_self = dot3(own_feat, w_self[...]) + bias[...]
    for axis, way in both:
        rs(axis, 0, way).wait_recv()
        first = coords[axis]
        n = spans[axis][1]
        mine = (0, 2) if way == 0 else (2, 2)
        far1[axis, way, :, pl.ds(0, n)] += line(axis, (first + ways[way] + SIDE) % SIDE, mine)[...]
        rs(axis, 2, way).start()
    for axis in (0, 1):
        for way in (0, 1):
            rs(axis, 1, way).wait_recv()
            rs(axis, 2, way).wait_recv()
        first, second = coords[axis], coords[1 - axis]
        lo, n = spans[axis]
        for off in (2, 1, 3, 0):
            at = (second + off) % SIDE
            y, x = index(axis, first, at)
            part1[axis, at, pl.ds(0, n)] = (
                sums[y, x, pl.ds(lo, n)] + near1[axis, 0, at, pl.ds(0, n)] + near1[axis, 1, at, pl.ds(0, n)]
            )
            if off == 2:
                for way in (0, 1):
                    rs(axis, 3, way).start()
    for axis in (0, 1):
        second = coords[1 - axis]
        n = spans[axis][1]
        cut = cuts[axis]
        for way in (0, 1):
            rs(axis, 3, way).wait_recv()
            at = (second + ways[way] + SIDE) % SIDE
            lo, size = (0, cut) if way == 0 else (cut, n - cut)
            part1[axis, at, pl.ds(lo, size)] += far2[axis, way, pl.ds(0, size)]
            rs(axis, 4, way).start()
    summed = []
    for axis in (0, 1):
        n = spans[axis][1]
        for way in (0, 1):
            rs(axis, 4, way).wait_recv()
        second = coords[1 - axis]
        summed.append(
            part1[axis, second, pl.ds(0, n)] + near2[axis, 0, pl.ds(0, n)] + near2[axis, 1, pl.ds(0, n)]
        )
    degree = summed[0][:1]
    inverse = 1.0 / jnp.maximum(degree, 1.0)
    inverse_down = jnp.broadcast_to(inverse, (block, block)).T
    total = jnp.concatenate([summed[0][DEG:], summed[1]], axis=0)
    aggregate = total * inverse_down
    preact = pre_self + dot3(aggregate, w_neigh[...])
    gating = jax.nn.sigmoid(preact)
    grad_pre = cot[rep] * (gating * (1.0 + preact * (1.0 - gating)))
    y0, x0 = coords[1], coords[0]
    gathered[y0, x0] = dot3(w_neigh[...], grad_pre, ((1,), (1,))) * inverse

    quarter = block // 4

    def place(axis, first, second):
        y, x = index(axis, first, second)
        return gathered.at[y, x]

    def ag(axis, kind, way, off=0, arrives=False):
        first, second = coords[axis], coords[1 - axis]
        w = ways[way]
        top = axis * (block // 2)
        if kind % 2 == 0:
            span = pl.ds(top, 2 * quarter)
        else:
            span = pl.ds(top + way * quarter, quarter)
        back = (kind % 2) + (1 if arrives else 0)
        if kind < 2:
            spot = place(axis, (first - w * back + 2 * SIDE) % SIDE, second)
            to = neighbour(axis, w)
            sems = (ag_send.at[axis, kind, way], ag_recv.at[axis, kind, way])
        else:
            spot = place(axis, (first + off) % SIDE, (second - w * back + 2 * SIDE) % SIDE)
            to = neighbour(1 - axis, w)
            at = 2 + (kind - 2) * SIDE + off
            sems = (ag_send.at[axis, at, way], ag_recv.at[axis, at, way])
        ref = spot.at[span]
        return remote(ref, ref, *sems, row=to)

    def convert(y, x):
        value = gathered[y, x]
        high, lo = split(value)
        stacked[y * SIDE + x, :, :block] = high
        stacked[y * SIDE + x, :, block:] = lo

    for axis, way in both:
        ag(axis, 0, way).start()
    for axis, way in both:
        ag(axis, 2, way, 0).start()
    hidden = preact * gating
    grad_self = dot3(own_feat.T, grad_pre)
    grad_neigh = dot3(aggregate.T, grad_pre)
    grad_bias = jnp.sum(grad_pre, axis=0, keepdims=True)
    share = 2 * width // rows
    for core in (0, 1):
        cols = slice(core * hid, (core + 1) * hid)
        hidden_half[core] = hidden[:, cols]
        grads[core, : rows // 2, :share] = grad_self[:, cols].reshape(rows // 2, share, hid)
        grads[core, rows // 2 :, :share] = grad_neigh[:, cols].reshape(rows // 2, share, hid)
        grads[core, :, share:] = jnp.broadcast_to(grad_bias[None, :, cols], (rows, 8, hid))
    grads_pair = remote(grads.at[other], grads_got, pair_send.at[0], pair_recv.at[0], rep=other)
    grads_pair.start()
    hidden_pair = remote(hidden_half.at[other], hidden_got, pair_send.at[1], pair_recv.at[1], rep=other)
    hidden_pair.start()
    for axis, way in both:
        ag(axis, 0, way, arrives=True).wait_recv()
        ag(axis, 1, way).start()
    for axis, way in both:
        off = 3 if way == 0 else 1
        for other_way in (0, 1):
            ag(axis, 2, other_way, off).start()
    direct = dot3(w_self[...], grad_pre, ((1,), (1,)))
    direct_half[...] = direct.reshape(2, width // 2, block)
    direct_pair = remote(direct_half.at[other], direct_got, pair_send.at[2], pair_recv.at[2], rep=other)
    direct_pair.start()
    grads_pair.wait_recv()
    grads[rep] += grads_got[...]
    for slot, peer in enumerate(peers):
        remote(
            grads.at[rep, peer], grads_rows.at[row], row_send.at[slot], row_recv.at[slot], row=peer
        ).start()
    grads_rows[row] = grads[rep, row]
    for axis, way in both:
        ag(axis, 1, way, arrives=True).wait_recv()
    for axis, way in both:
        ag(axis, 2, way, 2).start()
    for off in (0, 3, 1, 2):
        for axis, way in both:
            ag(axis, 2, way, off, arrives=True).wait_recv()
            ag(axis, 3, way, off).start()
    hidden_out[rep] = hidden_half[rep]
    hidden_pair.wait_recv()
    hidden_out[other] = hidden_got[...]
    direct_out[rep] = direct_half[rep]
    direct_pair.wait_recv()
    direct_out[other] = direct_got[...]
    for off in (0, 3, 1, 2):
        for axis, way in both:
            ag(axis, 3, way, off, arrives=True).wait_recv()
    for y in range(SIDE):
        for x in range(SIDE):
            convert(y, x)
    for slot in range(rows - 1):
        sender = (row + rows - (slot + 1)) % rows
        remote(
            grads.at[rep, row], grads_rows.at[sender], row_send.at[slot], row_recv.at[slot], row=peers[slot]
        ).wait_recv()
    value = grads_rows[0]
    for at in range(1, rows):
        value = value + grads_rows[at]
    grad_part[...] = value
    for axis, way in both:
        for kind in range(5):
            rs(axis, kind, way).wait_send()
        for kind in (0, 1):
            ag(axis, kind, way).wait_send()
        for off in range(SIDE):
            for kind in (2, 3):
                ag(axis, kind, way, off).wait_send()
    for copy in (grads_pair, hidden_pair, direct_pair):
        copy.wait_send()
    for slot, peer in enumerate(peers):
        remote(
            grads.at[rep, peer], grads_rows.at[row], row_send.at[slot], row_recv.at[slot], row=peer
        ).wait_send()


def middle(sums, feat, cot, w_self, w_neigh, bias):
    block, width = feat.shape[1:]
    hid = w_self.shape[1] // 2
    rows = SIDE * SIDE
    n = DEG + block // 2
    share = 2 * width // rows + 8
    vmem = pl.BlockSpec(memory_space=VMEM)
    shape = jax.ShapeDtypeStruct
    return pl.pallas_call(
        middle_kernel,
        out_shape=(
            shape((2, block, hid), F32),
            shape((rows, width, 2 * block), BF16),
            shape((2, width // 2, block), F32),
            shape((share, hid), F32),
        ),
        in_specs=[vmem] * 6,
        out_specs=(vmem,) * 4,
        scratch_shapes=[
            VMEM((2, 2, 2, n, width), F32),
            VMEM((2, 2, SIDE, n, width), F32),
            VMEM((2, SIDE, n, width), F32),
            VMEM((2, 2, n, width), F32),
            VMEM((2, 2, n, width), F32),
            VMEM((SIDE, SIDE, width, block), F32),
            VMEM((2, block, hid), F32),
            VMEM((block, hid), F32),
            VMEM((2, width // 2, block), F32),
            VMEM((width // 2, block), F32),
            VMEM((2, rows, share, hid), F32),
            VMEM((rows, share, hid), F32),
            VMEM((rows, share, hid), F32),
            DMA((2, 5, 2)),
            DMA((2, 5, 2)),
            DMA((2, 10, 2)),
            DMA((2, 10, 2)),
            DMA((3,)),
            DMA((3,)),
            DMA((rows - 1,)),
            DMA((rows - 1,)),
        ],
        compiler_params=pltpu.CompilerParams(
            collective_id=1, has_side_effects=True, vmem_limit_bytes=40 * MIB
        ),
        name="middle",
    )(sums, feat, cot, w_self, w_neigh, bias)


def last_kernel(
    cols, factor, sums, direct, grad_part,
    grad_feat, grad_weights, grad_bias,
    own, pair_got, ring_got, col_got, final,
    pair_send, pair_recv, ring_send, ring_recv, col_send, col_recv, row_send, row_recv,
):
    row = lax.axis_index("row")
    z = lax.axis_index("col")
    rep = lax.axis_index("rep")
    other = 1 - rep
    rows = SIDE * SIDE
    half = sums.shape[1] // 2
    share = final.shape[1]
    steps = cols // 2
    ways = (1, -1)
    row_peers = [(row + off) % rows for off in range(1, rows)]
    col_peers = [(z + off) % cols for off in range(1, cols)]
    greet(
        [{"rep": other}]
        + [{"col": peer} for peer in col_peers]
        + [{"row": peer} for peer in row_peers]
    )

    def pair(off):
        at = (z + off) % cols
        return remote(
            sums.at[pl.ds(2 * at, 2), pl.ds(other * half, half)], pair_got.at[at],
            pair_send.at[off], pair_recv.at[off], rep=other,
        )

    def merge(off):
        at = (z + off) % cols
        pair(off).wait_recv()
        own[at] = sums[pl.ds(2 * at, 2), pl.ds(pl.multiple_of(rep * half, half), half)] + pair_got[at]

    def ring(way, step, part):
        at = (z + ways[way] * (steps + 1 - step) + cols) % cols
        return remote(
            own.at[at, part], ring_got.at[way, step - 1, part],
            ring_send.at[way, step - 1, part], ring_recv.at[way, step - 1, part],
            col=(z + ways[way] + cols) % cols,
        )

    def to_col(slot, sender):
        return remote(
            grad_part, col_got.at[sender], col_send.at[slot], col_recv.at[slot], col=col_peers[slot]
        )

    def to_row(slot, sender):
        return remote(
            final.at[sender], final.at[sender], row_send.at[slot], row_recv.at[slot], row=row_peers[slot]
        )

    order = [steps]
    for off in range(steps - 1, 0, -1):
        order += [off, cols - off]
    order.append(0)
    for off in order:
        pair(off).start()
    for slot in range(cols - 1):
        to_col(slot, z).start()
    col_got[z] = grad_part[...]
    merge(steps)
    ring(0, 1, 0).start()
    ring(1, 1, 1).start()
    for step in range(2, steps + 1):
        off = steps + 1 - step
        for way in (0, 1):
            merge(off if way == 0 else cols - off)
        for part in (0, 1):
            for way in (0, 1):
                at = (z + ways[way] * off + cols) % cols
                if step > 2 or part == way:
                    ring(way, step - 1, part).wait_recv()
                    own[at, part] += ring_got[way, step - 2, part]
                ring(way, step, part).start()
        if step == 2:
            for slot in range(cols - 1):
                to_col(slot, (z + cols - (slot + 1)) % cols).wait_recv()
            value = col_got[0]
            for at in range(1, cols):
                value = value + col_got[at]
            value = value * factor
            final[row] = value[:share]
            grad_bias[...] = value[share:]
            for slot in range(rows - 1):
                to_row(slot, row).start()
    merge(0)
    for part in (0, 1):
        for way in (0, 1):
            ring(way, steps, part).wait_recv()
        grad_feat[part] = (
            direct[part] + own[z, part] + ring_got[0, steps - 1, part] + ring_got[1, steps - 1, part]
        )
    for slot in range(rows - 1):
        to_row(slot, (row + rows - (slot + 1)) % rows).wait_recv()
    grad_weights[...] = final[...]
    for off in order:
        pair(off).wait_send()
    for way in (0, 1):
        for step in range(1, steps + 1):
            for part in (0, 1):
                if step > 1 or part == way:
                    ring(way, step, part).wait_send()
    for slot in range(cols - 1):
        to_col(slot, z).wait_send()
    for slot in range(rows - 1):
        to_row(slot, row).wait_send()


def last(sums, direct, grad_part, cols, factor):
    width, block = sums.shape[1:]
    hid = grad_part.shape[1]
    rows = SIDE * SIDE
    share = 2 * width // rows
    vmem = pl.BlockSpec(memory_space=VMEM)
    shape = jax.ShapeDtypeStruct
    return pl.pallas_call(
        functools.partial(last_kernel, cols, factor),
        out_shape=(
            shape((2, width // 2, block), F32),
            shape((rows, share, hid), F32),
            shape((8, hid), F32),
        ),
        in_specs=[vmem] * 3,
        out_specs=(vmem,) * 3,
        scratch_shapes=[
            VMEM((cols, 2, width // 2, block), F32),
            VMEM((cols, 2, width // 2, block), F32),
            VMEM((2, cols // 2, 2, width // 2, block), F32),
            VMEM((cols, share + 8, hid), F32),
            VMEM((rows, share, hid), F32),
            DMA((cols,)),
            DMA((cols,)),
            DMA((2, cols // 2, 2)),
            DMA((2, cols // 2, 2)),
            DMA((cols - 1,)),
            DMA((cols - 1,)),
            DMA((rows - 1,)),
            DMA((rows - 1,)),
        ],
        compiler_params=pltpu.CompilerParams(
            collective_id=2, has_side_effects=True, vmem_limit_bytes=40 * MIB
        ),
        name="last",
    )(sums, direct, grad_part)


def shards(features, cotangent, w_self, w_neigh, bias, tiles, tile_dst, tile_src, tile_count):
    slots, block = tiles.shape[2:4]
    width = features.shape[1]
    hid = w_self.shape[1]
    cols = lax.axis_size("col")
    rows = lax.axis_size("row")
    tiles = tiles.reshape(slots, block, block)
    feat = features.reshape(2, block, width)
    cot = cotangent.reshape(2, block, hid)
    lists = (tile_count, tile_dst, tile_src, tiles)

    stacked = gather_features(feat, cols)
    sums = tile_call(
        forward_kernel, "forward", (SIDE + 1, SIDE, block + DEG, width),
        [VMEM((rows + 1, block, block), F32)], *lists, stacked,
    )
    hidden, scaled, direct, grad_part = middle(sums, feat, cot, w_self, w_neigh, bias.reshape(1, hid))
    back = tile_call(backward_kernel, "backward", (2 * cols + 1, width, block), [], *lists, scaled)
    factor = float(features.shape[0] * rows * cols) ** (-0.5)
    grad_feat, grad_weights, grad_bias = last(back, direct, grad_part, cols, factor)
    grad_weights = grad_weights.reshape(2, width, hid // 2)
    return (
        hidden.reshape(2 * block, hid // 2),
        grad_feat.transpose(0, 2, 1).reshape(2 * block, width // 2),
        grad_weights[0],
        grad_weights[1],
        grad_bias[0],
    )


def solution(mesh):
    return jax.shard_map(
        shards,
        mesh=mesh,
        in_specs=(
            P(("row", "col"), None),
            P(("row", "col"), None),
            P(),
            P(),
            P(),
            P("row", "col", None, None, None),
            P("row", "col", None),
            P("row", "col", None),
            P("row", "col"),
        ),
        out_specs=(
            P(("row", "col"), "rep"),
            P(("row", "col"), "rep"),
            P(None, "rep"),
            P(None, "rep"),
            P("rep"),
        ),
        check_vma=False,
    )
```

time: 684 us -> 118 us (0.17)
  the two profiles are of different devices: /device:TPU:0 before, /device:TPU:1 now
where the time goes in v1:
time: 118 us; the launch traced here: 117 us
  Pallas kernels  108 us (92%)
  local copies, waits for them, and re-layouts  7.82 us (7%)
  between operations  1.47 us (1%)
    pallas_call x2, Pallas kernels, tile_call(): pl.pallas_call(kernel, out_shape=jax.ShapeDtypeStruct(out_shape, F32), in...  33 us
    pallas_call x1, Pallas kernels, middle(): pl.pallas_call(middle_kernel, out_shape=(shape((2, block, hid), F32), sha...  30.5 us
    pallas_call x1, Pallas kernels, last(): pl.pallas_call(functools.partial(last_kernel, cols, factor), out_shape=(s...  23.1 us
    pallas_call x1, Pallas kernels, gather_features(): pl.pallas_call(functools.partial(gather_kernel, cols), out_shape=jax.Shap...  21.4 us
    unnamed x19, local copies, waits for them, and re-layouts  6.02 us

profile of v1, /device:TPU:1, one launch (start us, length us, event | category | flops | bytes accessed | tf_op | source)
XLA Modules:
  0.0 117.2 jit_solution(18422145801333274400)
XLA Ops:
  0.6 0.0 copy-start.7
  0.6 0.0 copy-start.6
  1.3 0.0 copy-start.1
  1.3 0.9 copy-done.1
  2.2 21.4 %gather_features.1.stacked = bf16[16,256,256]{2,1,0:T(8,128)(2,1)S(1)} custom-call(f32[2,128,128]{2,1,0:T(8,128)S(1)} %bitcast.17), custom_call_target="tpu_custom_call" | custom-call | tf_op jit(solution)/shard_map/gather_features/pallas_call | solution.py:135
  23.6 0.0 copy-done.7
  23.6 0.0 copy-done.6
  23.6 0.0 copy-start.2
  23.6 0.0 copy-start.3
  23.6 0.0 copy-start.4
  23.6 0.0 copy-start.5
  23.7 0.0 copy-start.8
  23.7 14.2 %forward.1.sums = f32[5,4,136,128]{3,2,1,0:T(8,128)S(1)} custom-call(s32[1,1]{1,0:T(1,128)S(6)} %copy.18.count, s32[1,1,184]{2,1,0:T(1,128)S(1)} %copy-done.6, s32[1,1,184]{2,1,0:T(1,128)S(1)} %copy-done.7, f32[184,128,128]{2,1,0:T(8,128)} %bitcast.15, bf16[16,256,256]{2,1,0:T(8,128)(2,1)S(1)} %gather_features.1.stacked), custom_call_target="tpu_custom_call" | custom-call | tf_op jit(solution)/shard_map/forward/pallas_call | solution.py:254
  37.9 0.0 copy-done.2
  37.9 0.0 copy-done.3
  37.9 0.0 copy-done.4
  37.9 0.0 copy-done.5
  37.9 0.0 copy-done.8
  37.9 30.5 %middle.1 = (f32[2,128,128]{2,1,0:T(8,128)S(1)}, bf16[16,128,256]{2,1,0:T(8,128)(2,1)S(1)}, f32[2,64,128]{2,1,0:T(8,128)S(1)}, f32[24,128]{1,0:T(8,128)S(1)}) custom-call(f32[5,4,136,128]{3,2,1,0:T(8,128)S(1)} %forward.1.sums, f32[2,128,128]{2,1,0:T(8,128)S(1)} %bitcast.18, f32[2,128,256]{2,1,0:T(8,128)S(1)} %bitcast.19, f32[128,256]{1,0:T(8,128)S(1)} %copy-done.4, ...), custom_call_target="tpu_custom_call" | custom-call | tf_op jit(solution)/shard_map/middle/pallas_call | solution.py:522
  68.4 0.0 copy-start
  68.4 4.4 %copy-done = f32[1,1,184,128,128]{4,3,2,1,0:T(8,128)S(1)} copy-done((f32[1,1,184,128,128]{4,3,2,1,0:T(8,128)S(1)}, f32[1,1,184,128,128]{4,3,2,1,0:T(8,128)}, u32[]{:S(2)}) %copy-start) | copy-done | bytes 12058648
  72.8 18.8 %backward.1.sums = f32[17,128,128]{2,1,0:T(8,128)S(1)} custom-call(s32[1,1]{1,0:T(1,128)S(6)} %copy.18.count, s32[1,1,184]{2,1,0:T(1,128)S(1)} %copy-done.6, s32[1,1,184]{2,1,0:T(1,128)S(1)} %copy-done.7, f32[184,128,128]{2,1,0:T(8,128)S(1)} %bitcast.16, bf16[16,128,256]{2,1,0:T(8,128)(2,1)S(1)} %get-tuple-element.13.stacked), custom_call_target="tpu_custom_call" | custom-call | tf_op jit(solution)/shard_map/backward/pallas_call | solution.py:254
  91.7 23.1 %last.1 = (f32[2,64,128]{2,1,0:T(8,128)S(1)}, f32[16,16,128]{2,1,0:T(8,128)S(1)}, f32[8,128]{1,0:T(8,128)S(1)}) custom-call(f32[17,128,128]{2,1,0:T(8,128)S(1)} %backward.1.sums, f32[2,64,128]{2,1,0:T(8,128)S(1)} %get-tuple-element.14.direct, f32[24,128]{1,0:T(8,128)S(1)} %get-tuple-element.15.grad_part), custom_call_target="tpu_custom_call" | custom-call | tf_op jit(solution)/shard_map/last/pallas_call | solution.py:679
  114.7 0.6 copy_bitcast_fusion
  115.4 0.5 slice_bitcast_fusion
  115.9 0.7 fusion
  116.6 0.7 copy.19
Async XLA Ops:
  0.6 23.0 %copy-start.7 = (s32[1,1,184]{2,1,0:T(1,128)S(1)}, s32[1,1,184]{2,1,0:T(1,128)}, u32[]{:S(2)}) copy-start(s32[1,1,184]{2,1,0:T(1,128)} %src.3) | copy-start | bytes 2212
  0.6 23.0 %copy-start.6 = (s32[1,1,184]{2,1,0:T(1,128)S(1)}, s32[1,1,184]{2,1,0:T(1,128)}, u32[]{:S(2)}) copy-start(s32[1,1,184]{2,1,0:T(1,128)} %dst.3) | copy-start | bytes 2212
  1.3 0.9 copy-start.1
  23.6 14.2 %copy-start.2 = (f32[256,128]{1,0:T(8,128)S(1)}, f32[256,128]{1,0:T(8,128)}, u32[]{:S(2)}) copy-start(f32[256,128]{1,0:T(8,128)} %param.9) | copy-start | bytes 393220
  23.6 14.2 %copy-start.3 = (f32[256,256]{1,0:T(8,128)S(1)}, f32[256,256]{1,0:T(8,128)}, u32[]{:S(2)}) copy-start(f32[256,256]{1,0:T(8,128)} %param.10) | copy-start | bytes 786436
  23.6 14.2 %copy-start.4 = (f32[128,256]{1,0:T(8,128)S(1)}, f32[128,256]{1,0:T(8,128)}, u32[]{:S(2)}) copy-start(f32[128,256]{1,0:T(8,128)} %w_self.1) | copy-start | bytes 393220
  23.6 14.2 %copy-start.5 = (f32[128,256]{1,0:T(8,128)S(1)}, f32[128,256]{1,0:T(8,128)}, u32[]{:S(2)}) copy-start(f32[128,256]{1,0:T(8,128)} %w_neigh.1) | copy-start | bytes 393220
  23.7 14.2 %copy-start.8 = (f32[256]{0:T(256)S(1)}, f32[256]{0:T(256)}, u32[]{:S(2)}) copy-start(f32[256]{0:T(256)} %param.13) | copy-start | bytes 3076
  68.4 4.4 %copy-start = (f32[1,1,184,128,128]{4,3,2,1,0:T(8,128)S(1)}, f32[1,1,184,128,128]{4,3,2,1,0:T(8,128)}, u32[]{:S(2)}) copy-start(f32[1,1,184,128,128]{4,3,2,1,0:T(8,128)} %param.14) | copy-start | bytes 36175876

commit v2 on v1

v2 whole, which is shorter than its diff:
```python
import functools

import jax
import jax.numpy as jnp
from jax import lax
from jax.experimental import pallas as pl
from jax.experimental.pallas import tpu as pltpu
from jax.sharding import PartitionSpec as P

MESH = pl.DeviceIdType.MESH
F32 = jnp.float32
BF16 = jnp.bfloat16
VMEM = pltpu.VMEM
DMA = pltpu.SemaphoreType.DMA
MIB = 1 << 20


def split(value):
    high = value.astype(BF16)
    low = (value - high.astype(F32)).astype(BF16)
    return high, low


def dot3(left, right, dims=((1,), (0,))):
    left_high, left_low = left if isinstance(left, tuple) else split(left)
    right_high, right_low = right if isinstance(right, tuple) else split(right)

    def one(a, b):
        return lax.dot_general(a, b, (dims, ((), ())), preferred_element_type=F32)

    return one(left_high, right_high) + (one(left_high, right_low) + one(left_low, right_high))


def remote(src, dst, send, recv, **where):
    return pltpu.make_async_remote_copy(
        src_ref=src, dst_ref=dst, send_sem=send, recv_sem=recv, device_id=where, device_id_type=MESH
    )


def greet(partners):
    barrier = pltpu.get_barrier_semaphore()
    for where in partners:
        pl.semaphore_signal(barrier, inc=1, device_id=where, device_id_type=MESH)
    pl.semaphore_wait(barrier, len(partners))


LIST = 256


def make_lists(count, dst, src, lists, line, dummies):
    rep = lax.axis_index("rep")
    slots = dst.shape[2]
    line[...] = jnp.zeros_like(line)
    line[0:1, :slots] = dst[0]
    line[8:9, :slots] = src[0]
    wide = (8, LIST)
    block = jnp.broadcast_to(line[0:1], wide)
    source = jnp.broadcast_to(line[8:9], wide)
    slot = lax.broadcasted_iota(jnp.int32, wide, 1)
    own = ((block & 1) == rep) & (slot < count[0, 0]) & (slot < slots)
    own = own.astype(jnp.int32).astype(F32)
    square = (LIST, LIST)
    down = lax.broadcasted_iota(jnp.int32, square, 0)
    before = (down < lax.broadcasted_iota(jnp.int32, square, 1)).astype(jnp.int32).astype(F32).astype(BF16)
    place = jnp.dot(own.astype(BF16), before, preferred_element_type=F32)
    place = jnp.where(own > 0.5, place, -1.0)
    total = jnp.broadcast_to(jnp.sum(own, axis=1, keepdims=True), wide)
    chosen = (jnp.broadcast_to(place[0:1], square) == down.astype(F32)).astype(jnp.int32).astype(F32).astype(BF16)
    kind = lax.broadcasted_iota(jnp.int32, wide, 0)
    values = jnp.where(kind == 0, slot, jnp.where(kind % 2 == 1, block >> 1, source)).astype(F32).astype(BF16)
    listed = lax.dot_general(values, chosen, (((1,), (1,)), ((), ())), preferred_element_type=F32)
    beyond = slot.astype(F32) >= total
    listed = jnp.where(beyond & (kind == 3), float(dummies[0]), listed)
    listed = jnp.where(beyond & (kind == 4), float(dummies[1]), listed)
    listed = jnp.where(kind == 5, total, listed)
    lists[...] = listed.astype(jnp.int32)


def gather_kernel(
    cols, dummies, count, dst_far, src_far, feat_far, tiles,
    stacked, lists, tiles_here,
    feat, dst, src, held, line, ring_send, ring_recv, pair_send, pair_recv, load_sems,
):
    loads = [
        pltpu.make_async_copy(far, here, load_sems.at[at])
        for at, (far, here) in enumerate(((feat_far, feat), (dst_far, dst), (src_far, src), (tiles, tiles_here)))
    ]
    for load in loads:
        load.start()
    z = lax.axis_index("col")
    rep = lax.axis_index("rep")
    other = 1 - rep
    half = feat.shape[1] // 2
    steps = cols // 2
    step_of = {0: 1, 1: -1}
    greet(({"col": (z + 1) % cols}, {"col": (z + cols - 1) % cols}, {"rep": other}))
    for load in loads[:3]:
        load.wait()

    def put(block, value):
        high, low = split(value)
        width = value.shape[1]
        stacked[block, :width, :width] = high
        stacked[block, :width, width:] = low
        stacked[block, width:, :width] = high
        stacked[block, width:, width:] = jnp.zeros_like(high)

    def rows(chunk):
        return pl.ds(chunk * half, half)

    def ring(way, step, chunk):
        origin = (z - step_of[way] * (step - 1) + cols) % cols
        dst = held.at[origin, rep, rows(chunk)]
        src = feat.at[rep, rows(chunk)] if step == 1 else dst
        return remote(
            src, dst, ring_send.at[way, step - 1, chunk], ring_recv.at[way, step - 1, chunk],
            col=(z + step_of[way] + cols) % cols,
        )

    def arrival(way, step, chunk):
        origin = (z - step_of[way] * step + cols) % cols
        dst = held.at[origin, rep, rows(chunk)]
        return remote(
            dst, dst, ring_send.at[way, step - 1, chunk], ring_recv.at[way, step - 1, chunk],
            col=(z + step_of[way] + cols) % cols,
        )

    def pair(way, step, chunk, core):
        origin = (z - step_of[way] * step + cols) % cols
        dst = held.at[origin, core, rows(chunk)]
        return remote(
            dst, dst, pair_send.at[way, step - 1, chunk], pair_recv.at[way, step - 1, chunk], rep=other
        )

    def messages(step):
        if step < steps:
            return [(way, chunk) for chunk in (0, 1) for way in (0, 1)]
        return [(0, 0), (1, 1)]

    for step in range(1, steps + 1):
        for way, chunk in messages(step):
            if step > 1:
                arrival(way, step - 1, chunk).wait_recv()
            ring(way, step, chunk).start()
            if step > 1:
                pair(way, step - 1, chunk, rep).start()
        if step > 1:
            for way, chunk in messages(step - 1):
                if (way, chunk) not in messages(step):
                    arrival(way, step - 1, chunk).wait_recv()
                    pair(way, step - 1, chunk, rep).start()
        if step == 1:
            for core in (0, 1):
                put(z * 2 + core, feat[core])
            make_lists(count, dst, src, lists, line, dummies)
        else:
            for way in (0, 1):
                origin = (z - step_of[way] * (step - 1) + cols) % cols
                put(origin * 2 + rep, held[origin, rep])
    for way, chunk in messages(steps):
        arrival(way, steps, chunk).wait_recv()
        pair(way, steps, chunk, rep).start()
    far = (z + steps) % cols
    put(far * 2 + rep, held[far, rep])
    for step in range(1, steps + 1):
        for way, chunk in messages(step):
            pair(way, step, chunk, other).wait_recv()
        for way in (0, 1) if step < steps else (0,):
            origin = (z - step_of[way] * step + cols) % cols
            put(origin * 2 + other, held[origin, other])
    for step in range(1, steps + 1):
        for way, chunk in messages(step):
            ring(way, step, chunk).wait_send()
            pair(way, step, chunk, rep).wait_send()
    loads[3].wait()


def gather_features(count, dst, src, feat, tiles, cols, rows):
    block, width = feat.shape[1:]
    sems = (2, cols // 2, 2)
    vmem = pl.BlockSpec(memory_space=VMEM)
    far = pl.BlockSpec(memory_space=pl.ANY)
    return pl.pallas_call(
        functools.partial(gather_kernel, cols, (rows, 2 * cols)),
        out_shape=(
            jax.ShapeDtypeStruct((cols * 2, 2 * width, 2 * width), BF16),
            jax.ShapeDtypeStruct((8, LIST), jnp.int32),
            VMEM(tiles.shape, F32),
        ),
        in_specs=[pl.BlockSpec(memory_space=pltpu.SMEM), far, far, far, far],
        out_specs=(vmem, vmem, vmem),
        scratch_shapes=[
            VMEM(feat.shape, F32), VMEM(dst.shape, jnp.int32), VMEM(src.shape, jnp.int32),
            VMEM((cols, 2, block, width), F32), VMEM((16, LIST), jnp.int32),
            DMA(sems), DMA(sems), DMA(sems), DMA(sems), DMA((4,)),
        ],
        compiler_params=pltpu.CompilerParams(
            collective_id=0, has_side_effects=True, vmem_limit_bytes=24 * MIB
        ),
        name="gather_features",
    )(*[pltpu.with_memory_space_constraint(x, pltpu.HBM) if x is not count else x for x in (count, dst, src, feat, tiles)])


UNROLL = 16
SLOT, LOAD_DST, LOAD_SRC, ADD_DST, ADD_SRC, TOTAL = range(6)


def group_count(lists):
    return (lists[TOTAL, 0] + (UNROLL - 1)) // UNROLL


def forward_kernel(lists, tiles, stacked, sums, weight):
    block = tiles.shape[1]
    live = sums.shape[0] - 1
    sums[...] = jnp.zeros_like(sums)
    weight[...] = jnp.zeros_like(weight)

    def step(group, carry):
        parts = []
        for u in range(UNROLL):
            place = group * UNROLL + u
            tile = tiles[lists[SLOT, place]]
            high, low = split(tile)
            product = jnp.dot(
                jnp.concatenate([high, low], axis=1), stacked[lists[LOAD_SRC, place]], preferred_element_type=F32
            )
            parts.append((lists[ADD_DST, place], product[:, :block] + product[:, block:], tile))
        for target, value, tile in parts:
            sums[target >> 2, target & 3, pl.ds(8, block)] += value
            weight[target] += tile
        return carry

    lax.fori_loop(0, group_count(lists), step, 0)
    ones = jnp.ones((8, block), F32)
    for target in range(4 * live):
        sums[target >> 2, target & 3, pl.ds(0, 8)] = lax.dot_general(
            ones, weight[target], (((1,), (1,)), ((), ())),
            precision=lax.Precision.HIGHEST, preferred_element_type=F32,
        )


def backward_kernel(lists, tiles, stacked, hidden, sums, hidden_out, out_sem):
    copy = pltpu.make_async_copy(hidden, hidden_out, out_sem)
    copy.start()
    block = tiles.shape[1]
    sums[...] = jnp.zeros_like(sums)

    def step(group, carry):
        parts = []
        for u in range(UNROLL):
            place = group * UNROLL + u
            high, low = split(tiles[lists[SLOT, place]])
            right = jnp.concatenate(
                [
                    jnp.concatenate([high, low], axis=1),
                    jnp.concatenate([high, jnp.zeros_like(high)], axis=1),
                ],
                axis=0,
            )
            product = jnp.dot(stacked[lists[LOAD_DST, place]], right, preferred_element_type=F32)
            parts.append((lists[ADD_SRC, place], product[:, :block] + product[:, block:]))
        for target, value in parts:
            sums[target] += value
        return carry

    lax.fori_loop(0, group_count(lists), step, 0)
    copy.wait()


def forward(lists, tiles, stacked, out_shape):
    vmem = pl.BlockSpec(memory_space=VMEM)
    block = tiles.shape[1]
    return pl.pallas_call(
        forward_kernel,
        out_shape=jax.ShapeDtypeStruct(out_shape, F32),
        in_specs=[pl.BlockSpec(memory_space=pltpu.SMEM), vmem, vmem],
        out_specs=vmem,
        scratch_shapes=[VMEM((4 * out_shape[0] - 3, block, block), F32)],
        compiler_params=pltpu.CompilerParams(vmem_limit_bytes=32 * MIB),
        name="forward",
    )(lists, tiles, stacked)


def backward(lists, tiles, stacked, hidden, out_shape):
    vmem = pl.BlockSpec(memory_space=VMEM)
    shape = jax.ShapeDtypeStruct
    return pl.pallas_call(
        backward_kernel,
        out_shape=(shape(out_shape, F32), shape(hidden.shape, F32)),
        in_specs=[pl.BlockSpec(memory_space=pltpu.SMEM), vmem, vmem, vmem],
        out_specs=(vmem, pl.BlockSpec(memory_space=pl.ANY)),
        scratch_shapes=[DMA],
        compiler_params=pltpu.CompilerParams(vmem_limit_bytes=32 * MIB),
        name="backward",
    )(lists, tiles, stacked, hidden)


SIDE = 4
DEG = 8


def middle_kernel(
    sums, feat, cot, w_self, w_neigh, bias,
    hidden_out, stacked, direct_out, grad_part,
    near1, part1, near2, gathered, hidden_half, hidden_got, direct_half, direct_got,
    grads, grads_got, grads_rows,
    rs_send, rs_recv, ag_send, ag_recv, pair_send, pair_recv, row_send, row_recv,
):
    row = lax.axis_index("row")
    rep = lax.axis_index("rep")
    other = 1 - rep
    rows = SIDE * SIDE
    block = feat.shape[1]
    width = feat.shape[2]
    hid = w_self.shape[1] // 2
    coords = (row % SIDE, row // SIDE)
    peers = [(row + off) % rows for off in range(1, rows)]
    greet([{"row": peer} for peer in peers] + [{"rep": other}])

    low = block // 2
    spans = ((0, DEG + low), (DEG + low, low))
    far_first = (2, 1, 3)

    def at(axis, first, second):
        one = (coords[axis] + first + SIDE) % SIDE
        two = (coords[1 - axis] + second + SIDE) % SIDE
        return (two, one) if axis == 0 else (one, two)

    def device(axis, first, second):
        y, x = at(axis, first, second)
        return y * SIDE + x

    def rs1(axis, off, line):
        lo, n = spans[axis]
        y, x = at(axis, off, line)
        return remote(
            sums.at[y, x, pl.ds(lo, n)], near1.at[axis, off - 1, line, pl.ds(0, n)],
            rs_send.at[axis, line, off - 1], rs_recv.at[axis, line, off - 1], row=device(axis, off, 0),
        )

    def rs2(axis, off):
        n = spans[axis][1]
        return remote(
            part1.at[axis, off, pl.ds(0, n)], near2.at[axis, off - 1, pl.ds(0, n)],
            rs_send.at[axis, SIDE, off - 1], rs_recv.at[axis, SIDE, off - 1], row=device(axis, 0, off),
        )

    lines = far_first + (0,)
    for line in lines:
        for off in far_first:
            for axis in (0, 1):
                rs1(axis, off, line).start()
    own_feat = split(feat[rep])
    self_parts = split(w_self[...])
    neigh_parts = split(w_neigh[...])
    pre_self = dot3(own_feat, self_parts) + bias[...]
    for line in lines:
        for axis in (0, 1):
            for off in far_first:
                rs1(axis, off, line).wait_recv()
            lo, n = spans[axis]
            y, x = at(axis, 0, line)
            span = pl.ds(0, n)
            part1[axis, line, span] = (sums[y, x, pl.ds(lo, n)] + near1[axis, 0, line, span]) + (
                near1[axis, 1, line, span] + near1[axis, 2, line, span]
            )
            if line:
                rs2(axis, line).start()
    summed = []
    for axis in (0, 1):
        for off in far_first:
            rs2(axis, off).wait_recv()
        span = pl.ds(0, spans[axis][1])
        summed.append(
            (part1[axis, 0, span] + near2[axis, 0, span]) + (near2[axis, 1, span] + near2[axis, 2, span])
        )
    degree = summed[0][:1]
    inverse = 1.0 / jnp.maximum(degree, 1.0)
    inverse_down = jnp.broadcast_to(inverse, (block, block)).T
    total = jnp.concatenate([summed[0][DEG:], summed[1]], axis=0)
    aggregate = total * inverse_down
    preact = pre_self + dot3(aggregate, neigh_parts)
    gating = jax.nn.sigmoid(preact)
    grad_pre = cot[rep] * (gating * (1.0 + preact * (1.0 - gating)))
    grad_parts = split(grad_pre)
    y0, x0 = coords[1], coords[0]
    scaled = dot3(neigh_parts, grad_parts, ((1,), (1,))) * inverse
    gathered[y0, x0] = scaled

    def half_of(axis, first, second):
        y, x = at(axis, first, second)
        return gathered.at[y, x, pl.ds(axis * low, low)]

    def ag1(axis, off, arrives=False):
        ref = half_of(axis, -off if arrives else 0, 0)
        return remote(
            ref, ref, ag_send.at[axis, 0, off - 1], ag_recv.at[axis, 0, off - 1], row=device(axis, off, 0)
        )

    def ag2(axis, back, off, arrives=False):
        ref = half_of(axis, -back, -off if arrives else 0)
        return remote(
            ref, ref, ag_send.at[axis, 1 + back, off - 1], ag_recv.at[axis, 1 + back, off - 1],
            row=device(axis, 0, off),
        )

    def convert(axis, first, second):
        y, x = at(axis, first, second)
        span = pl.ds(axis * low, low)
        high, small = split(gathered[y, x, span])
        stacked[y * SIDE + x, span, :block] = high
        stacked[y * SIDE + x, span, block:] = small

    for off in far_first:
        for axis in (0, 1):
            ag1(axis, off).start()
    for off in far_first:
        for axis in (0, 1):
            ag2(axis, 0, off).start()
    hidden = preact * gating
    for core in (0, 1):
        hidden_half[core] = hidden[:, core * hid : (core + 1) * hid]
    hidden_pair = remote(hidden_half.at[other], hidden_got, pair_send.at[1], pair_recv.at[1], rep=other)
    hidden_pair.start()
    grad_self = dot3(feat[rep].T, grad_parts)
    grad_neigh = dot3(aggregate.T, grad_parts)
    grad_bias = jnp.sum(grad_pre, axis=0, keepdims=True)
    share = 2 * width // rows
    for core in (0, 1):
        cols = slice(core * hid, (core + 1) * hid)
        grads[core, : rows // 2, :share] = grad_self[:, cols].reshape(rows // 2, share, hid)
        grads[core, rows // 2 :, :share] = grad_neigh[:, cols].reshape(rows // 2, share, hid)
        grads[core, :, share:] = jnp.broadcast_to(grad_bias[None, :, cols], (rows, 8, hid))
    grads_pair = remote(grads.at[other], grads_got, pair_send.at[0], pair_recv.at[0], rep=other)
    grads_pair.start()
    for off in (1, 3, 2):
        for axis in (0, 1):
            ag1(axis, off, arrives=True).wait_recv()
            for ahead in far_first:
                ag2(axis, off, ahead).start()
    direct = dot3(self_parts, grad_parts, ((1,), (1,)))
    direct_half[...] = direct.reshape(2, width // 2, block)
    direct_pair = remote(direct_half.at[other], direct_got, pair_send.at[2], pair_recv.at[2], rep=other)
    direct_pair.start()
    grads_pair.wait_recv()
    grads[rep] += grads_got[...]
    for slot, peer in enumerate(peers):
        remote(
            grads.at[rep, peer], grads_rows.at[row], row_send.at[slot], row_recv.at[slot], row=peer
        ).start()
    grads_rows[row] = grads[rep, row]
    hidden_out[rep] = hidden_half[rep]
    direct_out[rep] = direct_half[rep]
    for axis in (0, 1):
        for off in (0, 1, 3, 2):
            convert(axis, -off, 0)
    hidden_pair.wait_recv()
    hidden_out[other] = hidden_got[...]
    direct_pair.wait_recv()
    direct_out[other] = direct_got[...]
    for back in (0, 1, 3, 2):
        for ahead in (1, 3, 2):
            for axis in (0, 1):
                ag2(axis, back, ahead, arrives=True).wait_recv()
                convert(axis, -back, -ahead)
    for slot in range(rows - 1):
        sender = (row + rows - (slot + 1)) % rows
        remote(
            grads.at[rep, row], grads_rows.at[sender], row_send.at[slot], row_recv.at[slot], row=peers[slot]
        ).wait_recv()
    value = grads_rows[0]
    for place in range(1, rows):
        value = value + grads_rows[place]
    grad_part[...] = value
    for axis in (0, 1):
        for off in far_first:
            for line in lines:
                rs1(axis, off, line).wait_send()
                ag2(axis, line, off).wait_send()
            rs2(axis, off).wait_send()
            ag1(axis, off).wait_send()
    for copy in (grads_pair, hidden_pair, direct_pair):
        copy.wait_send()
    for slot, peer in enumerate(peers):
        remote(
            grads.at[rep, peer], grads_rows.at[row], row_send.at[slot], row_recv.at[slot], row=peer
        ).wait_send()


def middle(sums, feat, cot, w_self, w_neigh, bias):
    block, width = feat.shape[1:]
    hid = w_self.shape[1] // 2
    rows = SIDE * SIDE
    n = DEG + block // 2
    share = 2 * width // rows + 8
    vmem = pl.BlockSpec(memory_space=VMEM)
    shape = jax.ShapeDtypeStruct
    return pl.pallas_call(
        middle_kernel,
        out_shape=(
            shape((2, block, hid), F32),
            shape((rows, width, 2 * block), BF16),
            shape((2, width // 2, block), F32),
            shape((share, hid), F32),
        ),
        in_specs=[vmem] * 6,
        out_specs=(vmem,) * 4,
        scratch_shapes=[
            VMEM((2, SIDE - 1, SIDE, n, width), F32),
            VMEM((2, SIDE, n, width), F32),
            VMEM((2, SIDE - 1, n, width), F32),
            VMEM((SIDE, SIDE, width, block), F32),
            VMEM((2, block, hid), F32),
            VMEM((block, hid), F32),
            VMEM((2, width // 2, block), F32),
            VMEM((width // 2, block), F32),
            VMEM((2, rows, share, hid), F32),
            VMEM((rows, share, hid), F32),
            VMEM((rows, share, hid), F32),
            DMA((2, SIDE + 1, SIDE - 1)),
            DMA((2, SIDE + 1, SIDE - 1)),
            DMA((2, SIDE + 1, SIDE - 1)),
            DMA((2, SIDE + 1, SIDE - 1)),
            DMA((3,)),
            DMA((3,)),
            DMA((rows - 1,)),
            DMA((rows - 1,)),
        ],
        compiler_params=pltpu.CompilerParams(
            collective_id=1, has_side_effects=True, vmem_limit_bytes=20 * MIB
        ),
        name="middle",
    )(sums, feat, cot, w_self, w_neigh, bias)


def last_kernel(
    cols, factor, sums, direct, grad_part,
    grad_feat, grad_weights, grad_bias,
    own, pair_got, ring_got, col_got, final,
    pair_send, pair_recv, ring_send, ring_recv, col_send, col_recv, row_send, row_recv,
):
    row = lax.axis_index("row")
    z = lax.axis_index("col")
    rep = lax.axis_index("rep")
    other = 1 - rep
    rows = SIDE * SIDE
    half = sums.shape[1] // 2
    share = final.shape[1]
    steps = cols // 2
    ways = (1, -1)
    row_peers = [(row + off) % rows for off in range(1, rows)]
    col_peers = [(z + off) % cols for off in range(1, cols)]
    greet(
        [{"rep": other}]
        + [{"col": peer} for peer in col_peers]
        + [{"row": peer} for peer in row_peers]
    )

    def pair(off):
        at = (z + off) % cols
        return remote(
            sums.at[pl.ds(2 * at, 2), pl.ds(other * half, half)], pair_got.at[at],
            pair_send.at[off], pair_recv.at[off], rep=other,
        )

    def merge(off):
        at = (z + off) % cols
        pair(off).wait_recv()
        own[at] = sums[pl.ds(2 * at, 2), pl.ds(pl.multiple_of(rep * half, half), half)] + pair_got[at]

    def ring(way, step, part):
        at = (z + ways[way] * (steps + 1 - step) + cols) % cols
        return remote(
            own.at[at, part], ring_got.at[way, step - 1, part],
            ring_send.at[way, step - 1, part], ring_recv.at[way, step - 1, part],
            col=(z + ways[way] + cols) % cols,
        )

    def to_col(slot, sender):
        return remote(
            grad_part, col_got.at[sender], col_send.at[slot], col_recv.at[slot], col=col_peers[slot]
        )

    def to_row(slot, sender):
        return remote(
            final.at[sender], final.at[sender], row_send.at[slot], row_recv.at[slot], row=row_peers[slot]
        )

    order = [steps]
    for off in range(steps - 1, 0, -1):
        order += [off, cols - off]
    order.append(0)
    for off in order:
        pair(off).start()
    col_got[z] = grad_part[...]
    merge(steps)
    ring(0, 1, 0).start()
    ring(1, 1, 1).start()
    for slot in range(cols - 1):
        to_col(slot, z).start()
    for step in range(2, steps + 1):
        off = steps + 1 - step
        for way in (0, 1):
            merge(off if way == 0 else cols - off)
        for part in (0, 1):
            for way in (0, 1):
                at = (z + ways[way] * off + cols) % cols
                if step > 2 or part == way:
                    ring(way, step - 1, part).wait_recv()
                    own[at, part] += ring_got[way, step - 2, part]
                ring(way, step, part).start()
        if step == 3:
            for slot in range(cols - 1):
                to_col(slot, (z + cols - (slot + 1)) % cols).wait_recv()
            value = col_got[0]
            for at in range(1, cols):
                value = value + col_got[at]
            value = value * factor
            final[row] = value[:share]
            grad_bias[...] = value[share:]
            for slot in range(rows - 1):
                to_row(slot, row).start()
    merge(0)
    for part in (0, 1):
        for way in (0, 1):
            ring(way, steps, part).wait_recv()
        grad_feat[part] = (
            direct[part] + own[z, part] + ring_got[0, steps - 1, part] + ring_got[1, steps - 1, part]
        )
    for slot in range(rows - 1):
        to_row(slot, (row + rows - (slot + 1)) % rows).wait_recv()
    grad_weights[...] = final[...]
    for off in order:
        pair(off).wait_send()
    for way in (0, 1):
        for step in range(1, steps + 1):
            for part in (0, 1):
                if step > 1 or part == way:
                    ring(way, step, part).wait_send()
    for slot in range(cols - 1):
        to_col(slot, z).wait_send()
    for slot in range(rows - 1):
        to_row(slot, row).wait_send()


def last(sums, direct, grad_part, cols, factor):
    width, block = sums.shape[1:]
    hid = grad_part.shape[1]
    rows = SIDE * SIDE
    share = 2 * width // rows
    vmem = pl.BlockSpec(memory_space=VMEM)
    return pl.pallas_call(
        functools.partial(last_kernel, cols, factor),
        out_shape=(
            VMEM((2, width // 2, block), F32),
            VMEM((rows, share, hid), F32),
            VMEM((8, hid), F32),
        ),
        in_specs=[vmem] * 3,
        out_specs=(vmem,) * 3,
        scratch_shapes=[
            VMEM((cols, 2, width // 2, block), F32),
            VMEM((cols, 2, width // 2, block), F32),
            VMEM((2, cols // 2, 2, width // 2, block), F32),
            VMEM((cols, share + 8, hid), F32),
            VMEM((rows, share, hid), F32),
            DMA((cols,)),
            DMA((cols,)),
            DMA((2, cols // 2, 2)),
            DMA((2, cols // 2, 2)),
            DMA((cols - 1,)),
            DMA((cols - 1,)),
            DMA((rows - 1,)),
            DMA((rows - 1,)),
        ],
        compiler_params=pltpu.CompilerParams(
            collective_id=2, has_side_effects=True, vmem_limit_bytes=16 * MIB
        ),
        name="last",
    )(sums, direct, grad_part)


def finish_kernel(grad_feat, grad_weights, grad_bias, feat_out, self_out, neigh_out, bias_out, sems):
    block = grad_feat.shape[2]
    pieces = [
        (grad_feat.at[0], feat_out.at[:, pl.ds(0, block)]),
        (grad_feat.at[1], feat_out.at[:, pl.ds(block, block)]),
        (grad_weights.at[0], self_out),
        (grad_weights.at[1], neigh_out),
        (grad_bias.at[pl.ds(0, 1)], bias_out),
    ]
    copies = [pltpu.make_async_copy(src, dst, sems.at[at]) for at, (src, dst) in enumerate(pieces)]
    for copy in copies:
        copy.start()
    for copy in copies:
        copy.wait()


def finish(grad_feat, grad_weights, grad_bias):
    half, block = grad_feat.shape[1:]
    hid = grad_bias.shape[1]
    vmem = pl.BlockSpec(memory_space=VMEM)
    far = pl.BlockSpec(memory_space=pl.ANY)
    shape = jax.ShapeDtypeStruct
    return pl.pallas_call(
        finish_kernel,
        out_shape=(
            shape((half, 2 * block), F32), shape((2 * half, hid), F32), shape((2 * half, hid), F32), shape((1, hid), F32)
        ),
        in_specs=[vmem] * 3,
        out_specs=(far,) * 4,
        scratch_shapes=[DMA((5,))],
        name="finish",
    )(grad_feat, grad_weights.reshape(2, 2 * half, hid), grad_bias)


def shards(features, cotangent, w_self, w_neigh, bias, tiles, tile_dst, tile_src, tile_count):
    slots, block = tiles.shape[2:4]
    width = features.shape[1]
    hid = w_self.shape[1]
    cols = lax.axis_size("col")
    rows = lax.axis_size("row")
    tiles = tiles.reshape(slots, block, block)
    feat = features.reshape(2, block, width)
    cot = cotangent.reshape(2, block, hid)

    stacked, lists, tiles = gather_features(tile_count, tile_dst, tile_src, feat, tiles, cols, rows)
    sums = forward(lists, tiles, stacked, (SIDE + 1, SIDE, block + DEG, width))
    hidden, scaled, direct, grad_part = middle(sums, feat, cot, w_self, w_neigh, bias.reshape(1, hid))
    back, hidden = backward(lists, tiles, scaled, hidden, (2 * cols + 1, width, block))
    factor = float(features.shape[0] * rows * cols) ** (-0.5)
    grad_feat, grad_self, grad_neigh, grad_bias = finish(*last(back, direct, grad_part, cols, factor))
    return (
        hidden.reshape(2 * block, hid // 2), grad_feat.T, grad_self, grad_neigh, grad_bias.reshape(hid // 2)
    )


def solution(mesh):
    return jax.shard_map(
        shards,
        mesh=mesh,
        in_specs=(
            P(("row", "col"), None),
            P(("row", "col"), None),
            P(),
            P(),
            P(),
            P("row", "col", None, None, None),
            P("row", "col", None),
            P("row", "col", None),
            P("row", "col"),
        ),
        out_specs=(
            P(("row", "col"), "rep"),
            P(("row", "col"), "rep"),
            P(None, "rep"),
            P(None, "rep"),
            P("rep"),
        ),
        check_vma=False,
    )
```

time: 118 us -> 83.6 us (0.71)
  Pallas kernels: 108 us -> 80.2 us
  local copies, waits for them, and re-layouts: 7.82 us -> 1.89 us
    pallas_call x4 -> x5, Pallas kernels: 77.4 us -> 50.7 us  [the longest x1 21.6 us: gather_features(): pl.pallas_call(functools.partial(gather_kernel, cols, (rows, 2 * cols)),...]
    unnamed x19 -> x16, local copies, waits for them, and re-layouts: 6.02 us -> 1.89 us
where the time goes in v2:
time: 83.6 us; the launch traced here: 83.5 us
  Pallas kernels  80.2 us (96%)
  local copies, waits for them, and re-layouts  1.89 us (2%)
  between operations  1.39 us (2%)
    pallas_call x1, Pallas kernels, middle(): pl.pallas_call(middle_kernel, out_shape=(shape((2, block, hid), F32), sha...  29.5 us
    pallas_call x1, Pallas kernels, gather_features(): pl.pallas_call(functools.partial(gather_kernel, cols, (rows, 2 * cols)),...  21.6 us
    pallas_call x1, Pallas kernels, last(): pl.pallas_call(functools.partial(last_kernel, cols, factor), out_shape=(V...  21.3 us
    pallas_call x1, Pallas kernels, forward(): pl.pallas_call(forward_kernel, out_shape=jax.ShapeDtypeStruct(out_shape,...  4.11 us
    pallas_call x1, Pallas kernels, backward(): pl.pallas_call(backward_kernel, out_shape=(shape(out_shape, F32), shape(h...  2.15 us
    unnamed x16, local copies, waits for them, and re-layouts  1.89 us

profile of v2, /device:TPU:1, one launch (start us, length us, event | category | flops | bytes accessed | tf_op | source)
XLA Modules:
  0.0 83.5 jit_solution(1042476283594647637)
XLA Ops:
  1.3 21.6 %gather_features.1 = (bf16[16,256,256]{2,1,0:T(8,128)(2,1)S(1)}, s32[8,256]{1,0:T(8,128)S(1)}, f32[184,128,128]{2,1,0:T(8,128)S(1)}) custom-call(s32[1,1]{1,0:T(1,128)S(6)} %copy.14.count, s32[1,1,184]{2,1,0:T(1,128)} %dst_far.1, s32[1,1,184]{2,1,0:T(1,128)} %src_far.1, f32[2,128,128]{2,1,0:T(8,128)} %bitcast.8, f32[184,128,128]{2,1,0:T(8,128)} %bitcast.13), custom_call_target="tpu_custom_call" | custom-call | tf_op jit(solution)/shard_map/gather_features/pallas_call | solution.py:183
  22.9 0.0 copy-start
  22.9 0.0 copy-start.1
  22.9 0.0 copy-start.2
  22.9 0.0 copy-start.3
  22.9 0.0 copy-start.7
  22.9 4.1 %forward.1.sums = f32[5,4,136,128]{3,2,1,0:T(8,128)S(1)} custom-call(s32[8,256]{1,0:T(8,128)S(1)} %get-tuple-element.21.lists, f32[184,128,128]{2,1,0:T(8,128)S(1)} %get-tuple-element.22.tiles, bf16[16,256,256]{2,1,0:T(8,128)(2,1)S(1)} %get-tuple-element.23.stacked), custom_call_target="tpu_custom_call" | custom-call | tf_op jit(solution)/shard_map/forward/pallas_call | solution.py:273
  27.0 0.0 copy-done
  27.0 0.0 copy-done.1
  27.0 0.0 copy-done.2
  27.1 0.0 copy-done.3
  27.1 0.0 copy-done.7
  27.1 29.5 %middle.1 = (f32[2,128,128]{2,1,0:T(8,128)S(1)}, bf16[16,128,256]{2,1,0:T(8,128)(2,1)S(1)}, f32[2,64,128]{2,1,0:T(8,128)S(1)}, f32[24,128]{1,0:T(8,128)S(1)}) custom-call(f32[5,4,136,128]{3,2,1,0:T(8,128)S(1)} %forward.1.sums, f32[2,128,128]{2,1,0:T(8,128)S(1)} %bitcast.9, f32[2,128,256]{2,1,0:T(8,128)S(1)} %bitcast.10, f32[128,256]{1,0:T(8,128)S(1)} %copy-done.2, ...), custom_call_target="tpu_custom_call" | custom-call | tf_op jit(solution)/shard_map/middle/pallas_call | solution.py:498
  56.6 2.1 %backward.1 = (f32[17,128,128]{2,1,0:T(8,128)S(1)}, f32[2,128,128]{2,1,0:T(8,128)}) custom-call(s32[8,256]{1,0:T(8,128)S(1)} %get-tuple-element.21.lists, f32[184,128,128]{2,1,0:T(8,128)S(1)} %get-tuple-element.22.tiles, bf16[16,128,256]{2,1,0:T(8,128)(2,1)S(1)} %get-tuple-element.24.stacked, f32[2,128,128]{2,1,0:T(8,128)S(1)} %get-tuple-element.25.hidden), custom_call_target="tpu_custom_call" | custom-call | tf_op jit(solution)/shard_map/backward/pallas_call | solution.py:287
  58.7 21.3 %last.1 = (f32[2,64,128]{2,1,0:T(8,128)S(1)}, f32[16,16,128]{2,1,0:T(8,128)S(1)}, f32[8,128]{1,0:T(8,128)S(1)}) custom-call(f32[17,128,128]{2,1,0:T(8,128)S(1)} %get-tuple-element.27.sums, f32[2,64,128]{2,1,0:T(8,128)S(1)} %get-tuple-element.28.direct, f32[24,128]{1,0:T(8,128)S(1)} %get-tuple-element.29.grad_part), custom_call_target="tpu_custom_call" | custom-call | tf_op jit(solution)/shard_map/last/pallas_call | solution.py:652
  80.0 0.0 copy-start.4
  80.0 0.6 copy-done.4
  80.7 0.0 copy-start.5
  80.7 0.6 copy-done.5
  81.3 0.0 copy-start.6
  81.3 0.6 copy-done.6
  81.9 1.6 %finish.1 = (f32[64,256]{1,0:T(8,128)}, f32[128,128]{1,0:T(8,128)}, f32[128,128]{1,0:T(8,128)}, f32[1,128]{1,0:T(1,128)}) custom-call(f32[2,64,128]{2,1,0:T(8,128)} %copy-done.5, f32[2,128,128]{2,1,0:T(8,128)} %bitcast.11, f32[8,128]{1,0:T(8,128)} %copy-done.6), custom_call_target="tpu_custom_call" | custom-call | tf_op jit(solution)/shard_map/finish/pallas_call | solution.py:705
Async XLA Ops:
  22.9 4.2 %copy-start = (f32[256,128]{1,0:T(8,128)S(1)}, f32[256,128]{1,0:T(8,128)}, u32[]{:S(2)}) copy-start(f32[256,128]{1,0:T(8,128)} %param.9) | copy-start | bytes 393220
  22.9 4.2 %copy-start.1 = (f32[256,256]{1,0:T(8,128)S(1)}, f32[256,256]{1,0:T(8,128)}, u32[]{:S(2)}) copy-start(f32[256,256]{1,0:T(8,128)} %param.10) | copy-start | bytes 786436
  22.9 4.2 %copy-start.2 = (f32[128,256]{1,0:T(8,128)S(1)}, f32[128,256]{1,0:T(8,128)}, u32[]{:S(2)}) copy-start(f32[128,256]{1,0:T(8,128)} %w_self.1) | copy-start | bytes 393220
  22.9 4.2 %copy-start.3 = (f32[128,256]{1,0:T(8,128)S(1)}, f32[128,256]{1,0:T(8,128)}, u32[]{:S(2)}) copy-start(f32[128,256]{1,0:T(8,128)} %w_neigh.1) | copy-start | bytes 393220
  22.9 4.2 %copy-start.7 = (f32[256]{0:T(256)S(1)}, f32[256]{0:T(256)}, u32[]{:S(2)}) copy-start(f32[256]{0:T(256)} %param.13) | copy-start | bytes 3076
  80.0 0.7 copy-start.4
  80.7 0.6 copy-start.5
  81.3 0.6 copy-start.6

commit v3 on v2

--- a/solution.py
+++ b/solution.py
@@ -90,10 +90,9 @@
     z = lax.axis_index("col")
     rep = lax.axis_index("rep")
     other = 1 - rep
-    half = feat.shape[1] // 2
-    steps = cols // 2
-    step_of = {0: 1, 1: -1}
-    greet(({"col": (z + 1) % cols}, {"col": (z + cols - 1) % cols}, {"rep": other}))
+    rows = feat.shape[1]
+    ways = (1, -1)
+    greet([{"col": (z + off + cols) % cols} for off in (1, -1, 2, -2)] + [{"rep": other}])
     for load in loads[:3]:
         load.wait()
 
@@ -105,79 +104,76 @@
         stacked[block, width:, :width] = high
         stacked[block, width:, width:] = jnp.zeros_like(high)
 
-    def rows(chunk):
-        return pl.ds(chunk * half, half)
-
-    def ring(way, step, chunk):
-        origin = (z - step_of[way] * (step - 1) + cols) % cols
-        dst = held.at[origin, rep, rows(chunk)]
-        src = feat.at[rep, rows(chunk)] if step == 1 else dst
-        return remote(
-            src, dst, ring_send.at[way, step - 1, chunk], ring_recv.at[way, step - 1, chunk],
-            col=(z + step_of[way] + cols) % cols,
-        )
-
-    def arrival(way, step, chunk):
-        origin = (z - step_of[way] * step + cols) % cols
-        dst = held.at[origin, rep, rows(chunk)]
-        return remote(
-            dst, dst, ring_send.at[way, step - 1, chunk], ring_recv.at[way, step - 1, chunk],
-            col=(z + step_of[way] + cols) % cols,
-        )
-
-    def pair(way, step, chunk, core):
-        origin = (z - step_of[way] * step + cols) % cols
-        dst = held.at[origin, core, rows(chunk)]
-        return remote(
-            dst, dst, pair_send.at[way, step - 1, chunk], pair_recv.at[way, step - 1, chunk], rep=other
-        )
-
-    def messages(step):
-        if step < steps:
-            return [(way, chunk) for chunk in (0, 1) for way in (0, 1)]
-        return [(0, 0), (1, 1)]
-
-    for step in range(1, steps + 1):
-        for way, chunk in messages(step):
-            if step > 1:
-                arrival(way, step - 1, chunk).wait_recv()
-            ring(way, step, chunk).start()
-            if step > 1:
-                pair(way, step - 1, chunk, rep).start()
-        if step > 1:
-            for way, chunk in messages(step - 1):
-                if (way, chunk) not in messages(step):
-                    arrival(way, step - 1, chunk).wait_recv()
-                    pair(way, step - 1, chunk, rep).start()
-        if step == 1:
-            for core in (0, 1):
-                put(z * 2 + core, feat[core])
-            make_lists(count, dst, src, lists, line, dummies)
-        else:
-            for way in (0, 1):
-                origin = (z - step_of[way] * (step - 1) + cols) % cols
-                put(origin * 2 + rep, held[origin, rep])
-    for way, chunk in messages(steps):
-        arrival(way, steps, chunk).wait_recv()
-        pair(way, steps, chunk, rep).start()
-    far = (z + steps) % cols
-    put(far * 2 + rep, held[far, rep])
-    for step in range(1, steps + 1):
-        for way, chunk in messages(step):
-            pair(way, step, chunk, other).wait_recv()
-        for way in (0, 1) if step < steps else (0,):
-            origin = (z - step_of[way] * step + cols) % cols
-            put(origin * 2 + other, held[origin, other])
-    for step in range(1, steps + 1):
-        for way, chunk in messages(step):
-            ring(way, step, chunk).wait_send()
-            pair(way, step, chunk, rep).wait_send()
+    hops = (1, 2, 1, 2)
+
+    def spot(way, kind, core, steps):
+        origin = (z - ways[way] * steps + cols) % cols
+        if kind < 3:
+            return held.at[origin, core]
+        return held.at[origin, core, pl.ds(way * (rows // 2), rows // 2)]
+
+    def ring(way, kind, arrives=False):
+        back = 2 * (kind // 2)
+        dst = spot(way, kind, rep, back + (hops[kind] if arrives else 0))
+        src = feat.at[rep] if kind < 2 and not arrives else dst
+        return remote(
+            src, dst, ring_send.at[way, kind], ring_recv.at[way, kind],
+            col=(z + ways[way] * hops[kind] + cols) % cols,
+        )
+
+    def pair(way, kind, core):
+        dst = spot(way, kind, core, 2 * (kind // 2) + hops[kind])
+        return remote(dst, dst, pair_send.at[way, kind], pair_recv.at[way, kind], rep=other)
+
+    def take(kind, way, core):
+        steps = 2 * (kind // 2) + hops[kind]
+        origin = (z - ways[way] * steps + cols) % cols
+        put(origin * 2 + core, held[origin, core])
+
+    for kind in (1, 0):
+        for way in (0, 1):
+            ring(way, kind).start()
+    for way in (0, 1):
+        ring(way, 1, arrives=True).wait_recv()
+        for kind in (3, 2):
+            ring(way, kind).start()
+    for kind in (0, 1):
+        for way in (0, 1):
+            if kind == 0:
+                ring(way, kind, arrives=True).wait_recv()
+            pair(way, kind, rep).start()
+    for core in (0, 1):
+        put(z * 2 + core, feat[core])
+    make_lists(count, dst, src, lists, line, dummies)
+    for kind in (0, 1):
+        for way in (0, 1):
+            take(kind, way, rep)
+    for kind in (2, 3):
+        for way in (0, 1):
+            ring(way, kind, arrives=True).wait_recv()
+            pair(way, kind, rep).start()
+    for kind in (0, 1):
+        for way in (0, 1):
+            pair(way, kind, other).wait_recv()
+            take(kind, way, other)
+    for way in (0, 1):
+        take(2, way, rep)
+    take(3, 0, rep)
+    for kind in (2, 3):
+        for way in (0, 1):
+            pair(way, kind, other).wait_recv()
+            if kind == 2 or way == 1:
+                take(kind, way, other)
+    for kind in range(4):
+        for way in (0, 1):
+            ring(way, kind).wait_send()
+            pair(way, kind, rep).wait_send()
     loads[3].wait()
 
 
 def gather_features(count, dst, src, feat, tiles, cols, rows):
     block, width = feat.shape[1:]
-    sems = (2, cols // 2, 2)
+    sems = (2, 4)
     vmem = pl.BlockSpec(memory_space=VMEM)
     far = pl.BlockSpec(memory_space=pl.ANY)
     return pl.pallas_call(
@@ -201,12 +197,24 @@
     )(*[pltpu.with_memory_space_constraint(x, pltpu.HBM) if x is not count else x for x in (count, dst, src, feat, tiles)])
 
 
-UNROLL = 16
+LARGE, SMALL = 32, 8
 SLOT, LOAD_DST, LOAD_SRC, ADD_DST, ADD_SRC, TOTAL = range(6)
 
 
-def group_count(lists):
-    return (lists[TOTAL, 0] + (UNROLL - 1)) // UNROLL
+def over_tiles(lists, step):
+    total = lists[TOTAL, 0]
+    large = total // LARGE
+
+    def run(size, start):
+        def body(group, carry):
+            step(start + group * size, size)
+            return carry
+
+        return body
+
+    lax.fori_loop(0, large, run(LARGE, 0), 0)
+    rest = total - large * LARGE
+    lax.fori_loop(0, (rest + (SMALL - 1)) // SMALL, run(SMALL, large * LARGE), 0)
 
 
 def forward_kernel(lists, tiles, stacked, sums, weight):
@@ -215,10 +223,10 @@
     sums[...] = jnp.zeros_like(sums)
     weight[...] = jnp.zeros_like(weight)
 
-    def step(group, carry):
+    def step(start, size):
         parts = []
-        for u in range(UNROLL):
-            place = group * UNROLL + u
+        for u in range(size):
+            place = start + u
             tile = tiles[lists[SLOT, place]]
             high, low = split(tile)
             product = jnp.dot(
@@ -228,15 +236,11 @@
         for target, value, tile in parts:
             sums[target >> 2, target & 3, pl.ds(8, block)] += value
             weight[target] += tile
-        return carry
-
-    lax.fori_loop(0, group_count(lists), step, 0)
-    ones = jnp.ones((8, block), F32)
+
+    over_tiles(lists, step)
     for target in range(4 * live):
-        sums[target >> 2, target & 3, pl.ds(0, 8)] = lax.dot_general(
-            ones, weight[target], (((1,), (1,)), ((), ())),
-            precision=lax.Precision.HIGHEST, preferred_element_type=F32,
-        )
+        degree = jnp.sum(weight[target].T, axis=0, keepdims=True)
+        sums[target >> 2, target & 3, pl.ds(0, 8)] = jnp.broadcast_to(degree, (8, block))
 
 
 def backward_kernel(lists, tiles, stacked, hidden, sums, hidden_out, out_sem):
@@ -245,10 +249,10 @@
     block = tiles.shape[1]
     sums[...] = jnp.zeros_like(sums)
 
-    def step(group, carry):
+    def step(start, size):
         parts = []
-        for u in range(UNROLL):
-            place = group * UNROLL + u
+        for u in range(size):
+            place = start + u
             high, low = split(tiles[lists[SLOT, place]])
             right = jnp.concatenate(
                 [
@@ -261,9 +265,8 @@
             parts.append((lists[ADD_SRC, place], product[:, :block] + product[:, block:]))
         for target, value in parts:
             sums[target] += value
-        return carry
-
-    lax.fori_loop(0, group_count(lists), step, 0)
+
+    over_tiles(lists, step)
     copy.wait()
 
 
@@ -303,8 +306,8 @@
     sums, feat, cot, w_self, w_neigh, bias,
     hidden_out, stacked, direct_out, grad_part,
     near1, part1, near2, gathered, hidden_half, hidden_got, direct_half, direct_got,
-    grads, grads_got, grads_rows,
-    rs_send, rs_recv, ag_send, ag_recv, pair_send, pair_recv, row_send, row_recv,
+    grads, grads_got, grads_col,
+    rs_send, rs_recv, ag_send, ag_recv, pair_send, pair_recv, col_send, col_recv,
 ):
     row = lax.axis_index("row")
     rep = lax.axis_index("rep")
@@ -314,9 +317,6 @@
     width = feat.shape[2]
     hid = w_self.shape[1] // 2
     coords = (row % SIDE, row // SIDE)
-    peers = [(row + off) % rows for off in range(1, rows)]
-    greet([{"row": peer} for peer in peers] + [{"rep": other}])
-
     low = block // 2
     spans = ((0, DEG + low), (DEG + low, low))
     far_first = (2, 1, 3)
@@ -329,6 +329,15 @@
     def device(axis, first, second):
         y, x = at(axis, first, second)
         return y * SIDE + x
+
+    z = lax.axis_index("col")
+    cols = grads.shape[1]
+    around = (4, 3, 5, 2, 6, 1, 7)
+    greet(
+        [{"row": device(axis, off, 0)} for axis in (0, 1) for off in far_first]
+        + [{"col": (z + off) % cols} for off in around]
+        + [{"rep": other}]
+    )
 
     def rs1(axis, off, line):
         lo, n = spans[axis]
@@ -425,12 +434,12 @@
     grad_self = dot3(feat[rep].T, grad_parts)
     grad_neigh = dot3(aggregate.T, grad_parts)
     grad_bias = jnp.sum(grad_pre, axis=0, keepdims=True)
-    share = 2 * width // rows
+    share = 2 * width // cols
     for core in (0, 1):
-        cols = slice(core * hid, (core + 1) * hid)
-        grads[core, : rows // 2, :share] = grad_self[:, cols].reshape(rows // 2, share, hid)
-        grads[core, rows // 2 :, :share] = grad_neigh[:, cols].reshape(rows // 2, share, hid)
-        grads[core, :, share:] = jnp.broadcast_to(grad_bias[None, :, cols], (rows, 8, hid))
+        span = slice(core * hid, (core + 1) * hid)
+        grads[core, : cols // 2, :share] = grad_self[:, span].reshape(cols // 2, share, hid)
+        grads[core, cols // 2 :, :share] = grad_neigh[:, span].reshape(cols // 2, share, hid)
+        grads[core, :, share:] = jnp.broadcast_to(grad_bias[None, :, span], (cols, 8, hid))
     grads_pair = remote(grads.at[other], grads_got, pair_send.at[0], pair_recv.at[0], rep=other)
     grads_pair.start()
     for off in (1, 3, 2):
@@ -444,11 +453,16 @@
     direct_pair.start()
     grads_pair.wait_recv()
     grads[rep] += grads_got[...]
-    for slot, peer in enumerate(peers):
-        remote(
-            grads.at[rep, peer], grads_rows.at[row], row_send.at[slot], row_recv.at[slot], row=peer
-        ).start()
-    grads_rows[row] = grads[rep, row]
+
+    def to_col(off, arrives=False):
+        return remote(
+            grads.at[rep, (z + off) % cols], grads_col.at[(z + cols - off) % cols if arrives else z],
+            col_send.at[off - 1], col_recv.at[off - 1], col=(z + off) % cols,
+        )
+
+    for off in around:
+        to_col(off).start()
+    grads_col[z] = grads[rep, z]
     hidden_out[rep] = hidden_half[rep]
     direct_out[rep] = direct_half[rep]
     for axis in (0, 1):
@@ -463,14 +477,11 @@
             for axis in (0, 1):
                 ag2(axis, back, ahead, arrives=True).wait_recv()
                 convert(axis, -back, -ahead)
-    for slot in range(rows - 1):
-        sender = (row + rows - (slot + 1)) % rows
-        remote(
-            grads.at[rep, row], grads_rows.at[sender], row_send.at[slot], row_recv.at[slot], row=peers[slot]
-        ).wait_recv()
-    value = grads_rows[0]
-    for place in range(1, rows):
-        value = value + grads_rows[place]
+    for off in around:
+        to_col(off, arrives=True).wait_recv()
+    value = grads_col[0]
+    for place in range(1, cols):
+        value = value + grads_col[place]
     grad_part[...] = value
     for axis in (0, 1):
         for off in far_first:
@@ -479,20 +490,18 @@
                 ag2(axis, line, off).wait_send()
             rs2(axis, off).wait_send()
             ag1(axis, off).wait_send()
+    for off in around:
+        to_col(off).wait_send()
     for copy in (grads_pair, hidden_pair, direct_pair):
         copy.wait_send()
-    for slot, peer in enumerate(peers):
-        remote(
-            grads.at[rep, peer], grads_rows.at[row], row_send.at[slot], row_recv.at[slot], row=peer
-        ).wait_send()
-
-
-def middle(sums, feat, cot, w_self, w_neigh, bias):
+
+
+def middle(sums, feat, cot, w_self, w_neigh, bias, cols):
     block, width = feat.shape[1:]
     hid = w_self.shape[1] // 2
     rows = SIDE * SIDE
     n = DEG + block // 2
-    share = 2 * width // rows + 8
+    share = 2 * width // cols + 8
     vmem = pl.BlockSpec(memory_space=VMEM)
     shape = jax.ShapeDtypeStruct
     return pl.pallas_call(
@@ -514,17 +523,17 @@
             VMEM((block, hid), F32),
             VMEM((2, width // 2, block), F32),
             VMEM((width // 2, block), F32),
-            VMEM((2, rows, share, hid), F32),
-            VMEM((rows, share, hid), F32),
-            VMEM((rows, share, hid), F32),
+            VMEM((2, cols, share, hid), F32),
+            VMEM((cols, share, hid), F32),
+            VMEM((cols, share, hid), F32),
             DMA((2, SIDE + 1, SIDE - 1)),
             DMA((2, SIDE + 1, SIDE - 1)),
             DMA((2, SIDE + 1, SIDE - 1)),
             DMA((2, SIDE + 1, SIDE - 1)),
             DMA((3,)),
             DMA((3,)),
-            DMA((rows - 1,)),
-            DMA((rows - 1,)),
+            DMA((cols - 1,)),
+            DMA((cols - 1,)),
         ],
         compiler_params=pltpu.CompilerParams(
             collective_id=1, has_side_effects=True, vmem_limit_bytes=20 * MIB
@@ -536,124 +545,140 @@
 def last_kernel(
     cols, factor, sums, direct, grad_part,
     grad_feat, grad_weights, grad_bias,
-    own, pair_got, ring_got, col_got, final,
+    own, pair_got, got_one, got_two, got_three, got_four, got_x, line, got_y, final,
     pair_send, pair_recv, ring_send, ring_recv, col_send, col_recv, row_send, row_recv,
 ):
     row = lax.axis_index("row")
     z = lax.axis_index("col")
     rep = lax.axis_index("rep")
     other = 1 - rep
-    rows = SIDE * SIDE
     half = sums.shape[1] // 2
     share = final.shape[1]
-    steps = cols // 2
     ways = (1, -1)
-    row_peers = [(row + off) % rows for off in range(1, rows)]
-    col_peers = [(z + off) % cols for off in range(1, cols)]
+    x, y = row % SIDE, row // SIDE
+    far_first = (2, 1, 3)
+    x_peers = {off: y * SIDE + (x + off) % SIDE for off in far_first}
+    y_peers = {off: ((y + off) % SIDE) * SIDE + x for off in far_first}
     greet(
-        [{"rep": other}]
-        + [{"col": peer} for peer in col_peers]
-        + [{"row": peer} for peer in row_peers]
+        [{"col": (z + off) % cols} for off in range(1, cols)]
+        + [{"row": peer} for peer in list(x_peers.values()) + list(y_peers.values())]
+        + [{"rep": other}]
     )
 
+    def ahead(off):
+        return (z + off + 2 * cols) % cols
+
     def pair(off):
-        at = (z + off) % cols
+        at = ahead(off)
         return remote(
             sums.at[pl.ds(2 * at, 2), pl.ds(other * half, half)], pair_got.at[at],
-            pair_send.at[off], pair_recv.at[off], rep=other,
+            pair_send.at[off + 3], pair_recv.at[off + 3], rep=other,
         )
 
     def merge(off):
-        at = (z + off) % cols
+        at = ahead(off)
         pair(off).wait_recv()
         own[at] = sums[pl.ds(2 * at, 2), pl.ds(pl.multiple_of(rep * half, half), half)] + pair_got[at]
 
-    def ring(way, step, part):
-        at = (z + ways[way] * (steps + 1 - step) + cols) % cols
-        return remote(
-            own.at[at, part], ring_got.at[way, step - 1, part],
-            ring_send.at[way, step - 1, part], ring_recv.at[way, step - 1, part],
-            col=(z + ways[way] + cols) % cols,
-        )
-
-    def to_col(slot, sender):
-        return remote(
-            grad_part, col_got.at[sender], col_send.at[slot], col_recv.at[slot], col=col_peers[slot]
-        )
-
-    def to_row(slot, sender):
-        return remote(
-            final.at[sender], final.at[sender], row_send.at[slot], row_recv.at[slot], row=row_peers[slot]
-        )
-
-    order = [steps]
-    for off in range(steps - 1, 0, -1):
-        order += [off, cols - off]
-    order.append(0)
+    hops = (1, 2, 1, 2, 2)
+    got = (got_one, got_two, got_three, got_four, got_two)
+
+    def ring(way, kind):
+        at = ahead(ways[way] * (kind % 4 + 1 if kind < 4 else 2))
+        src, dst = own.at[at], got[kind].at[way]
+        if kind in (1, 3, 4):
+            part = 1 - way if kind == 4 else way
+            src = src.at[part]
+            if kind != 3:
+                dst = dst.at[part]
+        return remote(
+            src, dst, ring_send.at[way, kind], ring_recv.at[way, kind], col=ahead(ways[way] * hops[kind])
+        )
+
+    def to_x(off, arrives=False):
+        return remote(
+            grad_part, got_x.at[(x + SIDE - off) % SIDE if arrives else x],
+            row_send.at[0, off - 1], row_recv.at[0, off - 1], row=x_peers[off],
+        )
+
+    def to_y(off, arrives=False):
+        return remote(
+            line, got_y.at[(y + SIDE - off) % SIDE if arrives else y],
+            row_send.at[1, off - 1], row_recv.at[1, off - 1], row=y_peers[off],
+        )
+
+    def to_col(off, arrives=False):
+        ref = final.at[ahead(-off) if arrives else z]
+        return remote(ref, ref, col_send.at[off - 1], col_recv.at[off - 1], col=ahead(off))
+
+    order = (3, -3, 4, 1, -1, 2, -2, 0)
+    around = (4, 3, 5, 2, 6, 1, 7)
     for off in order:
         pair(off).start()
-    col_got[z] = grad_part[...]
-    merge(steps)
-    ring(0, 1, 0).start()
-    ring(1, 1, 1).start()
-    for slot in range(cols - 1):
-        to_col(slot, z).start()
-    for step in range(2, steps + 1):
-        off = steps + 1 - step
+    for off in far_first:
+        to_x(off).start()
+    got_x[x] = grad_part[...]
+    for off in order[:5]:
+        merge(off)
         for way in (0, 1):
-            merge(off if way == 0 else cols - off)
-        for part in (0, 1):
-            for way in (0, 1):
-                at = (z + ways[way] * off + cols) % cols
-                if step > 2 or part == way:
-                    ring(way, step - 1, part).wait_recv()
-                    own[at, part] += ring_got[way, step - 2, part]
-                ring(way, step, part).start()
-        if step == 3:
-            for slot in range(cols - 1):
-                to_col(slot, (z + cols - (slot + 1)) % cols).wait_recv()
-            value = col_got[0]
-            for at in range(1, cols):
-                value = value + col_got[at]
-            value = value * factor
-            final[row] = value[:share]
-            grad_bias[...] = value[share:]
-            for slot in range(rows - 1):
-                to_row(slot, row).start()
+            if off == 4 or off * ways[way] > 0:
+                ring(way, abs(off) - 1).start()
+    merge(2)
+    merge(-2)
+    for off in far_first:
+        to_x(off, arrives=True).wait_recv()
+    line[...] = (got_x[0] + got_x[1]) + (got_x[2] + got_x[3])
+    for off in far_first:
+        to_y(off).start()
+    got_y[y] = line[...]
+    for way in (0, 1):
+        ring(way, 2).wait_recv()
+        own[ahead(2 * ways[way])] += got_three[way]
+        ring(way, 4).start()
+    for way in (0, 1):
+        ring(way, 3).wait_recv()
+        own[ahead(2 * ways[way]), way] += got_four[way]
+        ring(way, 1).start()
     merge(0)
-    for part in (0, 1):
-        for way in (0, 1):
-            ring(way, steps, part).wait_recv()
-        grad_feat[part] = (
-            direct[part] + own[z, part] + ring_got[0, steps - 1, part] + ring_got[1, steps - 1, part]
-        )
-    for slot in range(rows - 1):
-        to_row(slot, (row + rows - (slot + 1)) % rows).wait_recv()
+    for off in far_first:
+        to_y(off, arrives=True).wait_recv()
+    value = ((got_y[0] + got_y[1]) + (got_y[2] + got_y[3])) * factor
+    final[z] = value[:share]
+    for off in around:
+        to_col(off).start()
+    grad_bias[...] = value[share:]
+    for way in (0, 1):
+        ring(way, 0).wait_recv()
+    grad_feat[...] = (direct[...] + own[z]) + (got_one[0] + got_one[1])
+    for way in (0, 1):
+        ring(way, 4).wait_recv()
+        ring(way, 1).wait_recv()
+    grad_feat[...] += got_two[0] + got_two[1]
+    for off in around:
+        to_col(off, arrives=True).wait_recv()
     grad_weights[...] = final[...]
     for off in order:
         pair(off).wait_send()
     for way in (0, 1):
-        for step in range(1, steps + 1):
-            for part in (0, 1):
-                if step > 1 or part == way:
-                    ring(way, step, part).wait_send()
-    for slot in range(cols - 1):
-        to_col(slot, z).wait_send()
-    for slot in range(rows - 1):
-        to_row(slot, row).wait_send()
+        for kind in range(5):
+            ring(way, kind).wait_send()
+    for off in around:
+        to_col(off).wait_send()
+    for off in far_first:
+        to_x(off).wait_send()
+        to_y(off).wait_send()
 
 
 def last(sums, direct, grad_part, cols, factor):
     width, block = sums.shape[1:]
     hid = grad_part.shape[1]
-    rows = SIDE * SIDE
-    share = 2 * width // rows
+    share = 2 * width // cols
     vmem = pl.BlockSpec(memory_space=VMEM)
     return pl.pallas_call(
         functools.partial(last_kernel, cols, factor),
         out_shape=(
             VMEM((2, width // 2, block), F32),
-            VMEM((rows, share, hid), F32),
+            VMEM((cols, share, hid), F32),
             VMEM((8, hid), F32),
         ),
         in_specs=[vmem] * 3,
@@ -661,17 +686,22 @@
         scratch_shapes=[
             VMEM((cols, 2, width // 2, block), F32),
             VMEM((cols, 2, width // 2, block), F32),
-            VMEM((2, cols // 2, 2, width // 2, block), F32),
-            VMEM((cols, share + 8, hid), F32),
-            VMEM((rows, share, hid), F32),
+            VMEM((2, 2, width // 2, block), F32),
+            VMEM((2, 2, width // 2, block), F32),
+            VMEM((2, 2, width // 2, block), F32),
+            VMEM((2, width // 2, block), F32),
+            VMEM((SIDE, share + 8, hid), F32),
+            VMEM((share + 8, hid), F32),
+            VMEM((SIDE, share + 8, hid), F32),
+            VMEM((cols, share, hid), F32),
             DMA((cols,)),
             DMA((cols,)),
-            DMA((2, cols // 2, 2)),
-            DMA((2, cols // 2, 2)),
+            DMA((2, 5)),
+            DMA((2, 5)),
             DMA((cols - 1,)),
             DMA((cols - 1,)),
-            DMA((rows - 1,)),
-            DMA((rows - 1,)),
+            DMA((2, SIDE - 1)),
+            DMA((2, SIDE - 1)),
         ],
         compiler_params=pltpu.CompilerParams(
             collective_id=2, has_side_effects=True, vmem_limit_bytes=16 * MIB
@@ -710,6 +740,7 @@
         in_specs=[vmem] * 3,
         out_specs=(far,) * 4,
         scratch_shapes=[DMA((5,))],
+        compiler_params=pltpu.CompilerParams(vmem_limit_bytes=8 * MIB),
         name="finish",
     )(grad_feat, grad_weights.reshape(2, 2 * half, hid), grad_bias)
 
@@ -726,7 +757,7 @@
 
     stacked, lists, tiles = gather_features(tile_count, tile_dst, tile_src, feat, tiles, cols, rows)
     sums = forward(lists, tiles, stacked, (SIDE + 1, SIDE, block + DEG, width))
-    hidden, scaled, direct, grad_part = middle(sums, feat, cot, w_self, w_neigh, bias.reshape(1, hid))
+    hidden, scaled, direct, grad_part = middle(sums, feat, cot, w_self, w_neigh, bias.reshape(1, hid), cols)
     back, hidden = backward(lists, tiles, scaled, hidden, (2 * cols + 1, width, block))
     factor = float(features.shape[0] * rows * cols) ** (-0.5)
     grad_feat, grad_self, grad_neigh, grad_bias = finish(*last(back, direct, grad_part, cols, factor))

time: 83.6 us -> 72.8 us (0.87)
  Pallas kernels: 80.2 us -> 71.2 us
  local copies, waits for them, and re-layouts: 1.89 us -> 0.03 us
    pallas_call x1, Pallas kernels: 29.5 us -> 26.1 us  [middle(): pl.pallas_call(middle_kernel, out_shape=(shape((2, block, hid), F32), sha...]
    pallas_call x1, Pallas kernels: 21.6 us -> 18.4 us  [gather_features(): pl.pallas_call(functools.partial(gather_kernel, cols, (rows, 2 * cols)),...]
    unnamed x16 -> x10, local copies, waits for them, and re-layouts: 1.89 us -> 0.03 us
    pallas_call x1, Pallas kernels: 21.3 us -> 20.1 us  [last(): pl.pallas_call(functools.partial(last_kernel, cols, factor), out_shape=(V...]
    pallas_call x1, Pallas kernels: 1.62 us -> 0.72 us  [finish(): pl.pallas_call(finish_kernel, out_shape=(shape((half, 2 * block), F32), s...]
where the time goes in v3:
time: 72.8 us; the launch traced here: 72.7 us
  Pallas kernels  71.2 us (98%)
  between operations  1.4 us (2%)
    pallas_call x1, Pallas kernels, middle(): pl.pallas_call(middle_kernel, out_shape=(shape((2, block, hid), F32), sha...  26.1 us
    pallas_call x1, Pallas kernels, last(): pl.pallas_call(functools.partial(last_kernel, cols, factor), out_shape=(V...  20.1 us
    pallas_call x1, Pallas kernels, gather_features(): pl.pallas_call(functools.partial(gather_kernel, cols, (rows, 2 * cols)),...  18.4 us
    pallas_call x1, Pallas kernels, forward(): pl.pallas_call(forward_kernel, out_shape=jax.ShapeDtypeStruct(out_shape,...  3.34 us
    pallas_call x1, Pallas kernels, backward(): pl.pallas_call(backward_kernel, out_shape=(shape(out_shape, F32), shape(h...  2.57 us

profile of v3, /device:TPU:1, one launch (start us, length us, event | category | flops | bytes accessed | tf_op | source)
XLA Modules:
  0.0 72.7 jit_solution(10337336814712346496)
XLA Ops:
  1.3 18.4 %gather_features.1 = (bf16[16,256,256]{2,1,0:T(8,128)(2,1)S(1)}, s32[8,256]{1,0:T(8,128)S(1)}, f32[184,128,128]{2,1,0:T(8,128)S(1)}) custom-call(s32[1,1]{1,0:T(1,128)S(6)} %copy.14.count, s32[1,1,184]{2,1,0:T(1,128)} %dst_far.1, s32[1,1,184]{2,1,0:T(1,128)} %src_far.1, f32[2,128,128]{2,1,0:T(8,128)} %bitcast.8, f32[184,128,128]{2,1,0:T(8,128)} %bitcast.13), custom_call_target="tpu_custom_call" | custom-call | tf_op jit(solution)/shard_map/gather_features/pallas_call | solution.py:179
  19.7 0.0 copy-start
  19.7 0.0 copy-start.1
  19.7 0.0 copy-start.2
  19.7 0.0 copy-start.3
  19.7 0.0 copy-start.4
  19.7 3.3 %forward.1.sums = f32[5,4,136,128]{3,2,1,0:T(8,128)S(1)} custom-call(s32[8,256]{1,0:T(8,128)S(1)} %get-tuple-element.21.lists, f32[184,128,128]{2,1,0:T(8,128)S(1)} %get-tuple-element.22.tiles, bf16[16,256,256]{2,1,0:T(8,128)(2,1)S(1)} %get-tuple-element.23.stacked), custom_call_target="tpu_custom_call" | custom-call | tf_op jit(solution)/shard_map/forward/pallas_call | solution.py:276
  23.1 0.0 copy-done
  23.1 0.0 copy-done.1
  23.1 0.0 copy-done.2
  23.1 0.0 copy-done.3
  23.1 0.0 copy-done.4
  23.1 26.1 %middle.1 = (f32[2,128,128]{2,1,0:T(8,128)S(1)}, bf16[16,128,256]{2,1,0:T(8,128)(2,1)S(1)}, f32[2,64,128]{2,1,0:T(8,128)S(1)}, f32[40,128]{1,0:T(8,128)S(1)}) custom-call(f32[5,4,136,128]{3,2,1,0:T(8,128)S(1)} %forward.1.sums, f32[2,128,128]{2,1,0:T(8,128)S(1)} %bitcast.9, f32[2,128,256]{2,1,0:T(8,128)S(1)} %bitcast.10, f32[128,256]{1,0:T(8,128)S(1)} %copy-done.2, ...), custom_call_target="tpu_custom_call" | custom-call | tf_op jit(solution)/shard_map/middle/pallas_call | solution.py:507
  49.2 2.6 %backward.1 = (f32[17,128,128]{2,1,0:T(8,128)S(1)}, f32[2,128,128]{2,1,0:T(8,128)}) custom-call(s32[8,256]{1,0:T(8,128)S(1)} %get-tuple-element.21.lists, f32[184,128,128]{2,1,0:T(8,128)S(1)} %get-tuple-element.22.tiles, bf16[16,128,256]{2,1,0:T(8,128)(2,1)S(1)} %get-tuple-element.24.stacked, f32[2,128,128]{2,1,0:T(8,128)S(1)} %get-tuple-element.25.hidden), custom_call_target="tpu_custom_call" | custom-call | tf_op jit(solution)/shard_map/backward/pallas_call | solution.py:290
  51.8 20.1 %last.1 = (f32[2,64,128]{2,1,0:T(8,128)S(1)}, f32[8,32,128]{2,1,0:T(8,128)S(1)}, f32[8,128]{1,0:T(8,128)S(1)}) custom-call(f32[17,128,128]{2,1,0:T(8,128)S(1)} %get-tuple-element.27.sums, f32[2,64,128]{2,1,0:T(8,128)S(1)} %get-tuple-element.28.direct, f32[40,128]{1,0:T(8,128)S(1)} %get-tuple-element.29.grad_part), custom_call_target="tpu_custom_call" | custom-call | tf_op jit(solution)/shard_map/last/pallas_call | solution.py:677
  71.9 0.7 finish.1
Async XLA Ops:
  19.7 3.4 %copy-start = (f32[256,128]{1,0:T(8,128)S(1)}, f32[256,128]{1,0:T(8,128)}, u32[]{:S(2)}) copy-start(f32[256,128]{1,0:T(8,128)} %param.9) | copy-start | bytes 393220
  19.7 3.4 %copy-start.1 = (f32[256,256]{1,0:T(8,128)S(1)}, f32[256,256]{1,0:T(8,128)}, u32[]{:S(2)}) copy-start(f32[256,256]{1,0:T(8,128)} %param.10) | copy-start | bytes 786436
  19.7 3.4 %copy-start.2 = (f32[128,256]{1,0:T(8,128)S(1)}, f32[128,256]{1,0:T(8,128)}, u32[]{:S(2)}) copy-start(f32[128,256]{1,0:T(8,128)} %w_self.1) | copy-start | bytes 393220
  19.7 3.4 %copy-start.3 = (f32[128,256]{1,0:T(8,128)S(1)}, f32[128,256]{1,0:T(8,128)}, u32[]{:S(2)}) copy-start(f32[128,256]{1,0:T(8,128)} %w_neigh.1) | copy-start | bytes 393220
  19.7 3.4 %copy-start.4 = (f32[256]{0:T(256)S(1)}, f32[256]{0:T(256)}, u32[]{:S(2)}) copy-start(f32[256]{0:T(256)} %param.13) | copy-start | bytes 3076

commit v4 on v3

--- a/solution.py
+++ b/solution.py
@@ -106,74 +106,83 @@
 
     hops = (1, 2, 1, 2)
 
-    def spot(way, kind, core, steps):
+    def spot(way, kind, core, steps, turn):
         origin = (z - ways[way] * steps + cols) % cols
-        if kind < 3:
-            return held.at[origin, core]
-        return held.at[origin, core, pl.ds(way * (rows // 2), rows // 2)]
-
-    def ring(way, kind, arrives=False):
+        part = way if turn == 0 else 1 - way
+        return held.at[origin, core, pl.ds(part * (rows // 2), rows // 2)]
+
+    def ring(way, kind, turn, arrives=False):
         back = 2 * (kind // 2)
-        dst = spot(way, kind, rep, back + (hops[kind] if arrives else 0))
-        src = feat.at[rep] if kind < 2 and not arrives else dst
-        return remote(
-            src, dst, ring_send.at[way, kind], ring_recv.at[way, kind],
+        dst = spot(way, kind, rep, back + (hops[kind] if arrives else 0), turn)
+        part = way if turn == 0 else 1 - way
+        src = feat.at[rep, pl.ds(part * (rows // 2), rows // 2)] if kind < 2 and not arrives else dst
+        return remote(
+            src, dst, ring_send.at[way, kind, turn], ring_recv.at[way, kind, turn],
             col=(z + ways[way] * hops[kind] + cols) % cols,
         )
 
-    def pair(way, kind, core):
-        dst = spot(way, kind, core, 2 * (kind // 2) + hops[kind])
-        return remote(dst, dst, pair_send.at[way, kind], pair_recv.at[way, kind], rep=other)
+    def pair(way, kind, turn, core):
+        dst = spot(way, kind, core, 2 * (kind // 2) + hops[kind], turn)
+        return remote(dst, dst, pair_send.at[way, kind, turn], pair_recv.at[way, kind, turn], rep=other)
 
     def take(kind, way, core):
         steps = 2 * (kind // 2) + hops[kind]
         origin = (z - ways[way] * steps + cols) % cols
         put(origin * 2 + core, held[origin, core])
 
+    both = (0, 1)
     for kind in (1, 0):
-        for way in (0, 1):
-            ring(way, kind).start()
-    for way in (0, 1):
-        ring(way, 1, arrives=True).wait_recv()
-        for kind in (3, 2):
-            ring(way, kind).start()
-    for kind in (0, 1):
-        for way in (0, 1):
-            if kind == 0:
-                ring(way, kind, arrives=True).wait_recv()
-            pair(way, kind, rep).start()
-    for core in (0, 1):
+        for turn in both:
+            for way in both:
+                ring(way, kind, turn).start()
+    for turn in both:
+        for way in both:
+            ring(way, 1, turn, arrives=True).wait_recv()
+            if turn == 0:
+                ring(way, 3, 0).start()
+            ring(way, 2, turn).start()
+            pair(way, 1, turn, rep).start()
+    for turn in both:
+        for way in both:
+            ring(way, 0, turn, arrives=True).wait_recv()
+            pair(way, 0, turn, rep).start()
+    for core in both:
         put(z * 2 + core, feat[core])
     make_lists(count, dst, src, lists, line, dummies)
     for kind in (0, 1):
-        for way in (0, 1):
+        for way in both:
             take(kind, way, rep)
-    for kind in (2, 3):
-        for way in (0, 1):
-            ring(way, kind, arrives=True).wait_recv()
-            pair(way, kind, rep).start()
-    for kind in (0, 1):
-        for way in (0, 1):
-            pair(way, kind, other).wait_recv()
+    for turn in both:
+        for kind in (2, 3) if turn == 0 else (2,):
+            for way in both:
+                ring(way, kind, turn, arrives=True).wait_recv()
+                pair(way, kind, turn, rep).start()
+    for kind in (1, 0):
+        for way in both:
+            for turn in both:
+                pair(way, kind, turn, other).wait_recv()
             take(kind, way, other)
-    for way in (0, 1):
+    for way in both:
         take(2, way, rep)
     take(3, 0, rep)
-    for kind in (2, 3):
-        for way in (0, 1):
-            pair(way, kind, other).wait_recv()
-            if kind == 2 or way == 1:
-                take(kind, way, other)
+    for way in both:
+        for turn in both:
+            pair(way, 2, turn, other).wait_recv()
+        take(2, way, other)
+    for way in both:
+        pair(way, 3, 0, other).wait_recv()
+    take(3, 0, other)
     for kind in range(4):
-        for way in (0, 1):
-            ring(way, kind).wait_send()
-            pair(way, kind, rep).wait_send()
+        for way in both:
+            for turn in both if kind < 3 else (0,):
+                ring(way, kind, turn).wait_send()
+                pair(way, kind, turn, rep).wait_send()
     loads[3].wait()
 
 
 def gather_features(count, dst, src, feat, tiles, cols, rows):
     block, width = feat.shape[1:]
-    sems = (2, 4)
+    sems = (2, 4, 2)
     vmem = pl.BlockSpec(memory_space=VMEM)
     far = pl.BlockSpec(memory_space=pl.ANY)
     return pl.pallas_call(
@@ -305,9 +314,9 @@
 def middle_kernel(
     sums, feat, cot, w_self, w_neigh, bias,
     hidden_out, stacked, direct_out, grad_part,
-    near1, part1, near2, gathered, hidden_half, hidden_got, direct_half, direct_got,
+    far1, near1, part1, near2, gathered, hidden_half, hidden_got, direct_half, direct_got,
     grads, grads_got, grads_col,
-    rs_send, rs_recv, ag_send, ag_recv, pair_send, pair_recv, col_send, col_recv,
+    rs_send, rs_recv, ag_send, ag_recv, pair_send, pair_recv, col_send, col_recv, near_in,
 ):
     row = lax.axis_index("row")
     rep = lax.axis_index("rep")
@@ -335,43 +344,74 @@
     around = (4, 3, 5, 2, 6, 1, 7)
     greet(
         [{"row": device(axis, off, 0)} for axis in (0, 1) for off in far_first]
-        + [{"col": (z + off) % cols} for off in around]
+        + [{"col": (z + off + cols) % cols} for off in (1, -1, 2, -2)]
         + [{"rep": other}]
     )
-
-    def rs1(axis, off, line):
+    for off in (2, -2):
+        pl.semaphore_signal(near_in, inc=1, device_id={"col": (z + off + cols) % cols}, device_id_type=MESH)
+
+    relay = {2: 0, 1: 0, 3: 1, 0: 1}
+    ways = (1, -1)
+
+    def rs0(axis, line):
         lo, n = spans[axis]
-        y, x = at(axis, off, line)
-        return remote(
-            sums.at[y, x, pl.ds(lo, n)], near1.at[axis, off - 1, line, pl.ds(0, n)],
-            rs_send.at[axis, line, off - 1], rs_recv.at[axis, line, off - 1], row=device(axis, off, 0),
+        y, x = at(axis, 2, line)
+        return remote(
+            sums.at[y, x, pl.ds(lo, n)], far1.at[axis, line, pl.ds(0, n)],
+            rs_send.at[axis, 0, line], rs_recv.at[axis, 0, line], row=device(axis, ways[relay[line]], 0),
+        )
+
+    def rs1(axis, way, line):
+        lo, n = spans[axis]
+        y, x = at(axis, ways[way], line)
+        if relay[line] == way:
+            src = far1.at[axis, line, pl.ds(0, n)]
+        else:
+            src = sums.at[y, x, pl.ds(lo, n)]
+        return remote(
+            src, near1.at[axis, way, line, pl.ds(0, n)],
+            rs_send.at[axis, 1 + way, line], rs_recv.at[axis, 1 + way, line], row=device(axis, ways[way], 0),
         )
 
     def rs2(axis, off):
         n = spans[axis][1]
         return remote(
             part1.at[axis, off, pl.ds(0, n)], near2.at[axis, off - 1, pl.ds(0, n)],
-            rs_send.at[axis, SIDE, off - 1], rs_recv.at[axis, SIDE, off - 1], row=device(axis, 0, off),
-        )
-
-    lines = far_first + (0,)
-    for line in lines:
-        for off in far_first:
-            for axis in (0, 1):
-                rs1(axis, off, line).start()
+            rs_send.at[axis, 3, off], rs_recv.at[axis, 3, off], row=device(axis, 0, off),
+        )
+
+    lines = (2, 3, 1, 0)
+    for line in (2, 3, 1):
+        for axis in (0, 1):
+            rs0(axis, line).start()
+    for line in (2, 3, 1):
+        for axis in (0, 1):
+            rs1(axis, 1 - relay[line], line).start()
+    for axis in (0, 1):
+        rs0(axis, 0).start()
     own_feat = split(feat[rep])
     self_parts = split(w_self[...])
     neigh_parts = split(w_neigh[...])
     pre_self = dot3(own_feat, self_parts) + bias[...]
     for line in lines:
         for axis in (0, 1):
-            for off in far_first:
-                rs1(axis, off, line).wait_recv()
+            rs0(axis, line).wait_recv()
+            way = relay[line]
+            lo, n = spans[axis]
+            y, x = at(axis, ways[way], line)
+            far1[axis, line, pl.ds(0, n)] += sums[y, x, pl.ds(lo, n)]
+            rs1(axis, way, line).start()
+            if line == 1:
+                rs1(axis, 1 - relay[0], 0).start()
+    for line in lines:
+        for axis in (0, 1):
+            for way in (0, 1):
+                rs1(axis, way, line).wait_recv()
             lo, n = spans[axis]
             y, x = at(axis, 0, line)
             span = pl.ds(0, n)
-            part1[axis, line, span] = (sums[y, x, pl.ds(lo, n)] + near1[axis, 0, line, span]) + (
-                near1[axis, 1, line, span] + near1[axis, 2, line, span]
+            part1[axis, line, span] = sums[y, x, pl.ds(lo, n)] + (
+                near1[axis, 0, line, span] + near1[axis, 1, line, span]
             )
             if line:
                 rs2(axis, line).start()
@@ -460,6 +500,7 @@
             col_send.at[off - 1], col_recv.at[off - 1], col=(z + off) % cols,
         )
 
+    pl.semaphore_wait(near_in, 2)
     for off in around:
         to_col(off).start()
     grads_col[z] = grads[rep, z]
@@ -485,11 +526,14 @@
     grad_part[...] = value
     for axis in (0, 1):
         for off in far_first:
-            for line in lines:
-                rs1(axis, off, line).wait_send()
-                ag2(axis, line, off).wait_send()
+            for back in range(SIDE):
+                ag2(axis, back, off).wait_send()
             rs2(axis, off).wait_send()
             ag1(axis, off).wait_send()
+        for line in lines:
+            rs0(axis, line).wait_send()
+            for way in (0, 1):
+                rs1(axis, way, line).wait_send()
     for off in around:
         to_col(off).wait_send()
     for copy in (grads_pair, hidden_pair, direct_pair):
@@ -515,7 +559,8 @@
         in_specs=[vmem] * 6,
         out_specs=(vmem,) * 4,
         scratch_shapes=[
-            VMEM((2, SIDE - 1, SIDE, n, width), F32),
+            VMEM((2, SIDE, n, width), F32),
+            VMEM((2, 2, SIDE, n, width), F32),
             VMEM((2, SIDE, n, width), F32),
             VMEM((2, SIDE - 1, n, width), F32),
             VMEM((SIDE, SIDE, width, block), F32),
@@ -526,14 +571,15 @@
             VMEM((2, cols, share, hid), F32),
             VMEM((cols, share, hid), F32),
             VMEM((cols, share, hid), F32),
-            DMA((2, SIDE + 1, SIDE - 1)),
-            DMA((2, SIDE + 1, SIDE - 1)),
+            DMA((2, 4, SIDE)),
+            DMA((2, 4, SIDE)),
             DMA((2, SIDE + 1, SIDE - 1)),
             DMA((2, SIDE + 1, SIDE - 1)),
             DMA((3,)),
             DMA((3,)),
             DMA((cols - 1,)),
             DMA((cols - 1,)),
+            pltpu.SemaphoreType.REGULAR,
         ],
         compiler_params=pltpu.CompilerParams(
             collective_id=1, has_side_effects=True, vmem_limit_bytes=20 * MIB
@@ -560,7 +606,7 @@
     x_peers = {off: y * SIDE + (x + off) % SIDE for off in far_first}
     y_peers = {off: ((y + off) % SIDE) * SIDE + x for off in far_first}
     greet(
-        [{"col": (z + off) % cols} for off in range(1, cols)]
+        [{"col": (z + off + cols) % cols} for off in (1, -1, 2, -2)]
         + [{"row": peer} for peer in list(x_peers.values()) + list(y_peers.values())]
         + [{"rep": other}]
     )

time: 72.8 us -> 71.5 us (0.982)
  Pallas kernels: 71.2 us -> 70 us
    pallas_call x1, Pallas kernels: 26.1 us -> 24.4 us  [middle(): pl.pallas_call(middle_kernel, out_shape=(shape((2, block, hid), F32), sha...]
where the time goes in v4:
time: 71.5 us; the launch traced here: 71.4 us
  Pallas kernels  70 us (98%)
  between operations  1.4 us (2%)
    pallas_call x1, Pallas kernels, middle(): pl.pallas_call(middle_kernel, out_shape=(shape((2, block, hid), F32), sha...  24.4 us
    pallas_call x1, Pallas kernels, last(): pl.pallas_call(functools.partial(last_kernel, cols, factor), out_shape=(V...  20.4 us
    pallas_call x1, Pallas kernels, gather_features(): pl.pallas_call(functools.partial(gather_kernel, cols, (rows, 2 * cols)),...  17.9 us
    pallas_call x1, Pallas kernels, forward(): pl.pallas_call(forward_kernel, out_shape=jax.ShapeDtypeStruct(out_shape,...  3.68 us
    pallas_call x1, Pallas kernels, backward(): pl.pallas_call(backward_kernel, out_shape=(shape(out_shape, F32), shape(h...  2.91 us

profile of v4, /device:TPU:1, one launch (start us, length us, event | category | flops | bytes accessed | tf_op | source)
XLA Modules:
  0.0 71.4 jit_solution(7624721383604797007)
XLA Ops:
  1.3 17.9 %gather_features.1 = (bf16[16,256,256]{2,1,0:T(8,128)(2,1)S(1)}, s32[8,256]{1,0:T(8,128)S(1)}, f32[184,128,128]{2,1,0:T(8,128)S(1)}) custom-call(s32[1,1]{1,0:T(1,128)S(6)} %copy.14.count, s32[1,1,184]{2,1,0:T(1,128)} %dst_far.1, s32[1,1,184]{2,1,0:T(1,128)} %src_far.1, f32[2,128,128]{2,1,0:T(8,128)} %bitcast.8, f32[184,128,128]{2,1,0:T(8,128)} %bitcast.13), custom_call_target="tpu_custom_call" | custom-call | tf_op jit(solution)/shard_map/gather_features/pallas_call | solution.py:188
  19.1 0.0 copy-start
  19.2 0.0 copy-start.1
  19.2 0.0 copy-start.2
  19.2 0.0 copy-start.3
  19.2 0.0 copy-start.4
  19.2 3.7 %forward.1.sums = f32[5,4,136,128]{3,2,1,0:T(8,128)S(1)} custom-call(s32[8,256]{1,0:T(8,128)S(1)} %get-tuple-element.21.lists, f32[184,128,128]{2,1,0:T(8,128)S(1)} %get-tuple-element.22.tiles, bf16[16,256,256]{2,1,0:T(8,128)(2,1)S(1)} %get-tuple-element.23.stacked), custom_call_target="tpu_custom_call" | custom-call | tf_op jit(solution)/shard_map/forward/pallas_call | solution.py:285
  22.9 0.0 copy-done
  22.9 0.0 copy-done.1
  22.9 0.0 copy-done.2
  22.9 0.0 copy-done.3
  22.9 0.0 copy-done.4
  22.9 24.4 %middle.1 = (f32[2,128,128]{2,1,0:T(8,128)S(1)}, bf16[16,128,256]{2,1,0:T(8,128)(2,1)S(1)}, f32[2,64,128]{2,1,0:T(8,128)S(1)}, f32[40,128]{1,0:T(8,128)S(1)}) custom-call(f32[5,4,136,128]{3,2,1,0:T(8,128)S(1)} %forward.1.sums, f32[2,128,128]{2,1,0:T(8,128)S(1)} %bitcast.9, f32[2,128,256]{2,1,0:T(8,128)S(1)} %bitcast.10, f32[128,256]{1,0:T(8,128)S(1)} %copy-done.2, ...), custom_call_target="tpu_custom_call" | custom-call | tf_op jit(solution)/shard_map/middle/pallas_call | solution.py:551
  47.4 2.9 %backward.1 = (f32[17,128,128]{2,1,0:T(8,128)S(1)}, f32[2,128,128]{2,1,0:T(8,128)}) custom-call(s32[8,256]{1,0:T(8,128)S(1)} %get-tuple-element.21.lists, f32[184,128,128]{2,1,0:T(8,128)S(1)} %get-tuple-element.22.tiles, bf16[16,128,256]{2,1,0:T(8,128)(2,1)S(1)} %get-tuple-element.24.stacked, f32[2,128,128]{2,1,0:T(8,128)S(1)} %get-tuple-element.25.hidden), custom_call_target="tpu_custom_call" | custom-call | tf_op jit(solution)/shard_map/backward/pallas_call | solution.py:299
  50.3 20.4 %last.1 = (f32[2,64,128]{2,1,0:T(8,128)S(1)}, f32[8,32,128]{2,1,0:T(8,128)S(1)}, f32[8,128]{1,0:T(8,128)S(1)}) custom-call(f32[17,128,128]{2,1,0:T(8,128)S(1)} %get-tuple-element.27.sums, f32[2,64,128]{2,1,0:T(8,128)S(1)} %get-tuple-element.28.direct, f32[40,128]{1,0:T(8,128)S(1)} %get-tuple-element.29.grad_part), custom_call_target="tpu_custom_call" | custom-call | tf_op jit(solution)/shard_map/last/pallas_call | solution.py:723
  70.7 0.7 %finish.1 = (f32[64,256]{1,0:T(8,128)}, f32[128,128]{1,0:T(8,128)}, f32[128,128]{1,0:T(8,128)}, f32[1,128]{1,0:T(1,128)}) custom-call(f32[2,64,128]{2,1,0:T(8,128)S(1)} %get-tuple-element.30.grad_feat, f32[2,128,128]{2,1,0:T(8,128)S(1)} %bitcast.11, f32[8,128]{1,0:T(8,128)S(1)} %get-tuple-element.32.grad_bias), custom_call_target="tpu_custom_call" | custom-call | tf_op jit(solution)/shard_map/finish/pallas_call | solution.py:781
Async XLA Ops:
  19.1 3.8 %copy-start = (f32[256,128]{1,0:T(8,128)S(1)}, f32[256,128]{1,0:T(8,128)}, u32[]{:S(2)}) copy-start(f32[256,128]{1,0:T(8,128)} %param.9) | copy-start | bytes 393220
  19.2 3.7 %copy-start.1 = (f32[256,256]{1,0:T(8,128)S(1)}, f32[256,256]{1,0:T(8,128)}, u32[]{:S(2)}) copy-start(f32[256,256]{1,0:T(8,128)} %param.10) | copy-start | bytes 786436
  19.2 3.7 %copy-start.2 = (f32[128,256]{1,0:T(8,128)S(1)}, f32[128,256]{1,0:T(8,128)}, u32[]{:S(2)}) copy-start(f32[128,256]{1,0:T(8,128)} %w_self.1) | copy-start | bytes 393220
  19.2 3.7 %copy-start.3 = (f32[128,256]{1,0:T(8,128)S(1)}, f32[128,256]{1,0:T(8,128)}, u32[]{:S(2)}) copy-start(f32[128,256]{1,0:T(8,128)} %w_neigh.1) | copy-start | bytes 393220
  19.2 3.7 %copy-start.4 = (f32[256]{0:T(256)S(1)}, f32[256]{0:T(256)}, u32[]{:S(2)}) copy-start(f32[256]{0:T(256)} %param.13) | copy-start | bytes 3076

commit v5 on v4

--- a/solution.py
+++ b/solution.py
@@ -131,10 +131,13 @@
         put(origin * 2 + core, held[origin, core])
 
     both = (0, 1)
-    for kind in (1, 0):
-        for turn in both:
-            for way in both:
-                ring(way, kind, turn).start()
+    for turn in both:
+        for way in both:
+            ring(way, 1, turn).start()
+    for turn in both:
+        for way in both:
+            ring(way, 1, turn).wait_send()
+            ring(way, 0, turn).start()
     for turn in both:
         for way in both:
             ring(way, 1, turn, arrives=True).wait_recv()
@@ -175,7 +178,8 @@
     for kind in range(4):
         for way in both:
             for turn in both if kind < 3 else (0,):
-                ring(way, kind, turn).wait_send()
+                if kind != 1:
+                    ring(way, kind, turn).wait_send()
                 pair(way, kind, turn, rep).wait_send()
     loads[3].wait()
 
@@ -343,12 +347,16 @@
     cols = grads.shape[1]
     around = (4, 3, 5, 2, 6, 1, 7)
     greet(
-        [{"row": device(axis, off, 0)} for axis in (0, 1) for off in far_first]
-        + [{"col": (z + off + cols) % cols} for off in (1, -1, 2, -2)]
+        [{"row": device(axis, off, 0)} for axis in (0, 1) for off in (1, -1)]
+        + [{"col": (z + off + cols) % cols} for off in (1, -1)]
         + [{"rep": other}]
     )
-    for off in (2, -2):
-        pl.semaphore_signal(near_in, inc=1, device_id={"col": (z + off + cols) % cols}, device_id_type=MESH)
+
+    def tell(reach):
+        for off in (reach, -reach):
+            pl.semaphore_signal(
+                near_in.at[reach - 1], inc=1, device_id={"col": (z + off + cols) % cols}, device_id_type=MESH
+            )
 
     relay = {2: 0, 1: 0, 3: 1, 0: 1}
     ways = (1, -1)
@@ -389,6 +397,7 @@
             rs1(axis, 1 - relay[line], line).start()
     for axis in (0, 1):
         rs0(axis, 0).start()
+    tell(1)
     own_feat = split(feat[rep])
     self_parts = split(w_self[...])
     neigh_parts = split(w_neigh[...])
@@ -403,6 +412,8 @@
             rs1(axis, way, line).start()
             if line == 1:
                 rs1(axis, 1 - relay[0], 0).start()
+    pl.semaphore_wait(near_in.at[0], 2)
+    tell(2)
     for line in lines:
         for axis in (0, 1):
             for way in (0, 1):
@@ -500,7 +511,7 @@
             col_send.at[off - 1], col_recv.at[off - 1], col=(z + off) % cols,
         )
 
-    pl.semaphore_wait(near_in, 2)
+    pl.semaphore_wait(near_in.at[1], 2)
     for off in around:
         to_col(off).start()
     grads_col[z] = grads[rep, z]
@@ -579,7 +590,7 @@
             DMA((3,)),
             DMA((cols - 1,)),
             DMA((cols - 1,)),
-            pltpu.SemaphoreType.REGULAR,
+            pltpu.SemaphoreType.REGULAR((2,)),
         ],
         compiler_params=pltpu.CompilerParams(
             collective_id=1, has_side_effects=True, vmem_limit_bytes=20 * MIB
@@ -592,7 +603,7 @@
     cols, factor, sums, direct, grad_part,
     grad_feat, grad_weights, grad_bias,
     own, pair_got, got_one, got_two, got_three, got_four, got_x, line, got_y, final,
-    pair_send, pair_recv, ring_send, ring_recv, col_send, col_recv, row_send, row_recv,
+    pair_send, pair_recv, ring_send, ring_recv, col_send, col_recv, row_send, row_recv, near_in,
 ):
     row = lax.axis_index("row")
     z = lax.axis_index("col")
@@ -605,11 +616,12 @@
     far_first = (2, 1, 3)
     x_peers = {off: y * SIDE + (x + off) % SIDE for off in far_first}
     y_peers = {off: ((y + off) % SIDE) * SIDE + x for off in far_first}
-    greet(
-        [{"col": (z + off + cols) % cols} for off in (1, -1, 2, -2)]
-        + [{"row": peer} for peer in list(x_peers.values()) + list(y_peers.values())]
-        + [{"rep": other}]
+    next_to = (
+        [{"col": (z + off + cols) % cols} for off in (1, -1)],
+        [{"row": x_peers[off]} for off in (1, 3)],
+        [{"row": y_peers[off]} for off in (1, 3)],
     )
+    greet(next_to[0] + next_to[1] + next_to[2] + [{"rep": other}])
 
     def ahead(off):
         return (z + off + 2 * cols) % cols
@@ -661,10 +673,17 @@
     around = (4, 3, 5, 2, 6, 1, 7)
     for off in order:
         pair(off).start()
-    for off in far_first:
+    for off in (1, 3):
         to_x(off).start()
+    for axis in range(3):
+        for where in next_to[axis]:
+            pl.semaphore_signal(near_in.at[axis], inc=1, device_id=where, device_id_type=MESH)
     got_x[x] = grad_part[...]
     for off in order[:5]:
+        if off == 4:
+            pl.semaphore_wait(near_in.at[0], 2)
+            pl.semaphore_wait(near_in.at[1], 2)
+            to_x(2).start()
         merge(off)
         for way in (0, 1):
             if off == 4 or off * ways[way] > 0:
@@ -674,6 +693,7 @@
     for off in far_first:
         to_x(off, arrives=True).wait_recv()
     line[...] = (got_x[0] + got_x[1]) + (got_x[2] + got_x[3])
+    pl.semaphore_wait(near_in.at[2], 2)
     for off in far_first:
         to_y(off).start()
     got_y[y] = line[...]
@@ -748,6 +768,7 @@
             DMA((cols - 1,)),
             DMA((2, SIDE - 1)),
             DMA((2, SIDE - 1)),
+            pltpu.SemaphoreType.REGULAR((3,)),
         ],
         compiler_params=pltpu.CompilerParams(
             collective_id=2, has_side_effects=True, vmem_limit_bytes=16 * MIB

time: 71.5 us -> 69.7 us (0.975)
  Pallas kernels: 70 us -> 68.2 us
    pallas_call x1, Pallas kernels: 20.4 us -> 19.4 us  [last(): pl.pallas_call(functools.partial(last_kernel, cols, factor), out_shape=(V...]
where the time goes in v5:
time: 69.7 us; the launch traced here: 69.6 us
  Pallas kernels  68.2 us (98%)
  between operations  1.4 us (2%)
    pallas_call x1, Pallas kernels, middle(): pl.pallas_call(middle_kernel, out_shape=(shape((2, block, hid), F32), sha...  24.6 us
    pallas_call x1, Pallas kernels, last(): pl.pallas_call(functools.partial(last_kernel, cols, factor), out_shape=(V...  19.4 us
    pallas_call x1, Pallas kernels, gather_features(): pl.pallas_call(functools.partial(gather_kernel, cols, (rows, 2 * cols)),...  17.9 us
    pallas_call x1, Pallas kernels, forward(): pl.pallas_call(forward_kernel, out_shape=jax.ShapeDtypeStruct(out_shape,...  3.1 us
    pallas_call x1, Pallas kernels, backward(): pl.pallas_call(backward_kernel, out_shape=(shape(out_shape, F32), shape(h...  2.48 us

profile of v5, /device:TPU:1, one launch (start us, length us, event | category | flops | bytes accessed | tf_op | source)
XLA Modules:
  0.0 69.6 jit_solution(10707420505738366666)
XLA Ops:
  1.3 17.9 %gather_features.1 = (bf16[16,256,256]{2,1,0:T(8,128)(2,1)S(1)}, s32[8,256]{1,0:T(8,128)S(1)}, f32[184,128,128]{2,1,0:T(8,128)S(1)}) custom-call(s32[1,1]{1,0:T(1,128)S(6)} %copy.14.count, s32[1,1,184]{2,1,0:T(1,128)} %dst_far.1, s32[1,1,184]{2,1,0:T(1,128)} %src_far.1, f32[2,128,128]{2,1,0:T(8,128)} %bitcast.8, f32[184,128,128]{2,1,0:T(8,128)} %bitcast.13), custom_call_target="tpu_custom_call" | custom-call | tf_op jit(solution)/shard_map/gather_features/pallas_call | solution.py:192
  19.1 0.0 copy-start
  19.2 0.0 copy-start.1
  19.2 0.0 copy-start.2
  19.2 0.0 copy-start.3
  19.2 0.0 copy-start.4
  19.2 3.1 %forward.1.sums = f32[5,4,136,128]{3,2,1,0:T(8,128)S(1)} custom-call(s32[8,256]{1,0:T(8,128)S(1)} %get-tuple-element.21.lists, f32[184,128,128]{2,1,0:T(8,128)S(1)} %get-tuple-element.22.tiles, bf16[16,256,256]{2,1,0:T(8,128)(2,1)S(1)} %get-tuple-element.23.stacked), custom_call_target="tpu_custom_call" | custom-call | tf_op jit(solution)/shard_map/forward/pallas_call | solution.py:289
  22.3 0.0 copy-done
  22.3 0.0 copy-done.1
  22.3 0.0 copy-done.2
  22.3 0.0 copy-done.3
  22.4 0.0 copy-done.4
  22.4 24.6 %middle.1 = (f32[2,128,128]{2,1,0:T(8,128)S(1)}, bf16[16,128,256]{2,1,0:T(8,128)(2,1)S(1)}, f32[2,64,128]{2,1,0:T(8,128)S(1)}, f32[40,128]{1,0:T(8,128)S(1)}) custom-call(f32[5,4,136,128]{3,2,1,0:T(8,128)S(1)} %forward.1.sums, f32[2,128,128]{2,1,0:T(8,128)S(1)} %bitcast.9, f32[2,128,256]{2,1,0:T(8,128)S(1)} %bitcast.10, f32[128,256]{1,0:T(8,128)S(1)} %copy-done.2, ...), custom_call_target="tpu_custom_call" | custom-call | tf_op jit(solution)/shard_map/middle/pallas_call | solution.py:562
  46.9 2.5 %backward.1 = (f32[17,128,128]{2,1,0:T(8,128)S(1)}, f32[2,128,128]{2,1,0:T(8,128)}) custom-call(s32[8,256]{1,0:T(8,128)S(1)} %get-tuple-element.21.lists, f32[184,128,128]{2,1,0:T(8,128)S(1)} %get-tuple-element.22.tiles, bf16[16,128,256]{2,1,0:T(8,128)(2,1)S(1)} %get-tuple-element.24.stacked, f32[2,128,128]{2,1,0:T(8,128)S(1)} %get-tuple-element.25.hidden), custom_call_target="tpu_custom_call" | custom-call | tf_op jit(solution)/shard_map/backward/pallas_call | solution.py:303
  49.4 19.4 %last.1 = (f32[2,64,128]{2,1,0:T(8,128)S(1)}, f32[8,32,128]{2,1,0:T(8,128)S(1)}, f32[8,128]{1,0:T(8,128)S(1)}) custom-call(f32[17,128,128]{2,1,0:T(8,128)S(1)} %get-tuple-element.27.sums, f32[2,64,128]{2,1,0:T(8,128)S(1)} %get-tuple-element.28.direct, f32[40,128]{1,0:T(8,128)S(1)} %get-tuple-element.29.grad_part), custom_call_target="tpu_custom_call" | custom-call | tf_op jit(solution)/shard_map/last/pallas_call | solution.py:743
  68.9 0.7 %finish.1 = (f32[64,256]{1,0:T(8,128)}, f32[128,128]{1,0:T(8,128)}, f32[128,128]{1,0:T(8,128)}, f32[1,128]{1,0:T(1,128)}) custom-call(f32[2,64,128]{2,1,0:T(8,128)S(1)} %get-tuple-element.30.grad_feat, f32[2,128,128]{2,1,0:T(8,128)S(1)} %bitcast.11, f32[8,128]{1,0:T(8,128)S(1)} %get-tuple-element.32.grad_bias), custom_call_target="tpu_custom_call" | custom-call | tf_op jit(solution)/shard_map/finish/pallas_call | solution.py:802
Async XLA Ops:
  19.1 3.2 %copy-start = (f32[256,128]{1,0:T(8,128)S(1)}, f32[256,128]{1,0:T(8,128)}, u32[]{:S(2)}) copy-start(f32[256,128]{1,0:T(8,128)} %param.9) | copy-start | bytes 393220
  19.2 3.2 %copy-start.1 = (f32[256,256]{1,0:T(8,128)S(1)}, f32[256,256]{1,0:T(8,128)}, u32[]{:S(2)}) copy-start(f32[256,256]{1,0:T(8,128)} %param.10) | copy-start | bytes 786436
  19.2 3.2 %copy-start.2 = (f32[128,256]{1,0:T(8,128)S(1)}, f32[128,256]{1,0:T(8,128)}, u32[]{:S(2)}) copy-start(f32[128,256]{1,0:T(8,128)} %w_self.1) | copy-start | bytes 393220
  19.2 3.2 %copy-start.3 = (f32[128,256]{1,0:T(8,128)S(1)}, f32[128,256]{1,0:T(8,128)}, u32[]{:S(2)}) copy-start(f32[128,256]{1,0:T(8,128)} %w_neigh.1) | copy-start | bytes 393220
  19.2 3.2 %copy-start.4 = (f32[256]{0:T(256)S(1)}, f32[256]{0:T(256)}, u32[]{:S(2)}) copy-start(f32[256]{0:T(256)} %param.13) | copy-start | bytes 3076

commit v6 on v5

--- a/solution.py
+++ b/solution.py
@@ -168,6 +168,14 @@
     for way in both:
         take(2, way, rep)
     take(3, 0, rep)
+    loads[3].wait()
+    for way in both:
+        for turn in both:
+            for kind in (0, 2):
+                ring(way, kind, turn).wait_send()
+            for kind in (0, 1):
+                pair(way, kind, turn, rep).wait_send()
+        ring(way, 3, 0).wait_send()
     for way in both:
         for turn in both:
             pair(way, 2, turn, other).wait_recv()
@@ -175,13 +183,10 @@
     for way in both:
         pair(way, 3, 0, other).wait_recv()
     take(3, 0, other)
-    for kind in range(4):
+    for kind in (2, 3):
         for way in both:
             for turn in both if kind < 3 else (0,):
-                if kind != 1:
-                    ring(way, kind, turn).wait_send()
                 pair(way, kind, turn, rep).wait_send()
-    loads[3].wait()
 
 
 def gather_features(count, dst, src, feat, tiles, cols, rows):
@@ -524,6 +529,16 @@
     hidden_out[other] = hidden_got[...]
     direct_pair.wait_recv()
     direct_out[other] = direct_got[...]
+    for axis in (0, 1):
+        for line in lines:
+            rs0(axis, line).wait_send()
+            for way in (0, 1):
+                rs1(axis, way, line).wait_send()
+        for off in far_first:
+            rs2(axis, off).wait_send()
+            ag1(axis, off).wait_send()
+    for copy in (grads_pair, hidden_pair, direct_pair):
+        copy.wait_send()
     for back in (0, 1, 3, 2):
         for ahead in (1, 3, 2):
             for axis in (0, 1):
@@ -539,16 +554,8 @@
         for off in far_first:
             for back in range(SIDE):
                 ag2(axis, back, off).wait_send()
-            rs2(axis, off).wait_send()
-            ag1(axis, off).wait_send()
-        for line in lines:
-            rs0(axis, line).wait_send()
-            for way in (0, 1):
-                rs1(axis, way, line).wait_send()
     for off in around:
         to_col(off).wait_send()
-    for copy in (grads_pair, hidden_pair, direct_pair):
-        copy.wait_send()
 
 
 def middle(sums, feat, cot, w_self, w_neigh, bias, cols):
@@ -716,6 +723,14 @@
     for way in (0, 1):
         ring(way, 0).wait_recv()
     grad_feat[...] = (direct[...] + own[z]) + (got_one[0] + got_one[1])
+    for off in order:
+        pair(off).wait_send()
+    for way in (0, 1):
+        for kind in (0, 2, 3):
+            ring(way, kind).wait_send()
+    for off in far_first:
+        to_x(off).wait_send()
+        to_y(off).wait_send()
     for way in (0, 1):
         ring(way, 4).wait_recv()
         ring(way, 1).wait_recv()
@@ -723,16 +738,11 @@
     for off in around:
         to_col(off, arrives=True).wait_recv()
     grad_weights[...] = final[...]
-    for off in order:
-        pair(off).wait_send()
     for way in (0, 1):
-        for kind in range(5):
+        for kind in (1, 4):
             ring(way, kind).wait_send()
     for off in around:
         to_col(off).wait_send()
-    for off in far_first:
-        to_x(off).wait_send()
-        to_y(off).wait_send()
 
 
 def last(sums, direct, grad_part, cols, factor):

time: 69.7 us -> 69 us (0.990); the launches traced: 69.6 us -> 68.2 us
  Pallas kernels: 68.2 us -> 66.7 us
    pallas_call x1, Pallas kernels: 19.4 us -> 18.3 us  [last(): pl.pallas_call(functools.partial(last_kernel, cols, factor), out_shape=(V...]
where the time goes in v6:
time: 69 us; the launch traced here: 68.2 us
  Pallas kernels  66.7 us (97%)
  between operations  1.4 us (2%)
    pallas_call x1, Pallas kernels, middle(): pl.pallas_call(middle_kernel, out_shape=(shape((2, block, hid), F32), sha...  24 us
    pallas_call x1, Pallas kernels, last(): pl.pallas_call(functools.partial(last_kernel, cols, factor), out_shape=(V...  18.3 us
    pallas_call x1, Pallas kernels, gather_features(): pl.pallas_call(functools.partial(gather_kernel, cols, (rows, 2 * cols)),...  17.8 us
    pallas_call x1, Pallas kernels, forward(): pl.pallas_call(forward_kernel, out_shape=jax.ShapeDtypeStruct(out_shape,...  3.34 us
    pallas_call x1, Pallas kernels, backward(): pl.pallas_call(backward_kernel, out_shape=(shape(out_shape, F32), shape(h...  2.58 us

profile of v6, /device:TPU:1, one launch (start us, length us, event | category | flops | bytes accessed | tf_op | source)
XLA Modules:
  0.0 68.2 jit_solution(6110634524639937286)
XLA Ops:
  1.3 17.8 %gather_features.1 = (bf16[16,256,256]{2,1,0:T(8,128)(2,1)S(1)}, s32[8,256]{1,0:T(8,128)S(1)}, f32[184,128,128]{2,1,0:T(8,128)S(1)}) custom-call(s32[1,1]{1,0:T(1,128)S(6)} %copy.14.count, s32[1,1,184]{2,1,0:T(1,128)} %dst_far.1, s32[1,1,184]{2,1,0:T(1,128)} %src_far.1, f32[2,128,128]{2,1,0:T(8,128)} %bitcast.8, f32[184,128,128]{2,1,0:T(8,128)} %bitcast.13), custom_call_target="tpu_custom_call" | custom-call | tf_op jit(solution)/shard_map/gather_features/pallas_call | solution.py:197
  19.1 0.0 copy-start
  19.1 0.0 copy-start.1
  19.1 0.0 copy-start.2
  19.1 0.0 copy-start.3
  19.2 0.0 copy-start.4
  19.2 3.3 %forward.1.sums = f32[5,4,136,128]{3,2,1,0:T(8,128)S(1)} custom-call(s32[8,256]{1,0:T(8,128)S(1)} %get-tuple-element.21.lists, f32[184,128,128]{2,1,0:T(8,128)S(1)} %get-tuple-element.22.tiles, bf16[16,256,256]{2,1,0:T(8,128)(2,1)S(1)} %get-tuple-element.23.stacked), custom_call_target="tpu_custom_call" | custom-call | tf_op jit(solution)/shard_map/forward/pallas_call | solution.py:294
  22.5 0.0 copy-done
  22.5 0.0 copy-done.1
  22.5 0.0 copy-done.2
  22.5 0.0 copy-done.3
  22.6 0.0 copy-done.4
  22.6 24.0 %middle.1 = (f32[2,128,128]{2,1,0:T(8,128)S(1)}, bf16[16,128,256]{2,1,0:T(8,128)(2,1)S(1)}, f32[2,64,128]{2,1,0:T(8,128)S(1)}, f32[40,128]{1,0:T(8,128)S(1)}) custom-call(f32[5,4,136,128]{3,2,1,0:T(8,128)S(1)} %forward.1.sums, f32[2,128,128]{2,1,0:T(8,128)S(1)} %bitcast.9, f32[2,128,256]{2,1,0:T(8,128)S(1)} %bitcast.10, f32[128,256]{1,0:T(8,128)S(1)} %copy-done.2, ...), custom_call_target="tpu_custom_call" | custom-call | tf_op jit(solution)/shard_map/middle/pallas_call | solution.py:569
  46.6 2.6 %backward.1 = (f32[17,128,128]{2,1,0:T(8,128)S(1)}, f32[2,128,128]{2,1,0:T(8,128)}) custom-call(s32[8,256]{1,0:T(8,128)S(1)} %get-tuple-element.21.lists, f32[184,128,128]{2,1,0:T(8,128)S(1)} %get-tuple-element.22.tiles, bf16[16,128,256]{2,1,0:T(8,128)(2,1)S(1)} %get-tuple-element.24.stacked, f32[2,128,128]{2,1,0:T(8,128)S(1)} %get-tuple-element.25.hidden), custom_call_target="tpu_custom_call" | custom-call | tf_op jit(solution)/shard_map/backward/pallas_call | solution.py:308
  49.2 18.3 %last.1 = (f32[2,64,128]{2,1,0:T(8,128)S(1)}, f32[8,32,128]{2,1,0:T(8,128)S(1)}, f32[8,128]{1,0:T(8,128)S(1)}) custom-call(f32[17,128,128]{2,1,0:T(8,128)S(1)} %get-tuple-element.27.sums, f32[2,64,128]{2,1,0:T(8,128)S(1)} %get-tuple-element.28.direct, f32[40,128]{1,0:T(8,128)S(1)} %get-tuple-element.29.grad_part), custom_call_target="tpu_custom_call" | custom-call | tf_op jit(solution)/shard_map/last/pallas_call | solution.py:753
  67.4 0.7 %finish.1 = (f32[64,256]{1,0:T(8,128)}, f32[128,128]{1,0:T(8,128)}, f32[128,128]{1,0:T(8,128)}, f32[1,128]{1,0:T(1,128)}) custom-call(f32[2,64,128]{2,1,0:T(8,128)S(1)} %get-tuple-element.30.grad_feat, f32[2,128,128]{2,1,0:T(8,128)S(1)} %bitcast.11, f32[8,128]{1,0:T(8,128)S(1)} %get-tuple-element.32.grad_bias), custom_call_target="tpu_custom_call" | custom-call | tf_op jit(solution)/shard_map/finish/pallas_call | solution.py:812
Async XLA Ops:
  19.1 3.4 %copy-start = (f32[256,128]{1,0:T(8,128)S(1)}, f32[256,128]{1,0:T(8,128)}, u32[]{:S(2)}) copy-start(f32[256,128]{1,0:T(8,128)} %param.9) | copy-start | bytes 393220
  19.1 3.4 %copy-start.1 = (f32[256,256]{1,0:T(8,128)S(1)}, f32[256,256]{1,0:T(8,128)}, u32[]{:S(2)}) copy-start(f32[256,256]{1,0:T(8,128)} %param.10) | copy-start | bytes 786436
  19.1 3.4 %copy-start.2 = (f32[128,256]{1,0:T(8,128)S(1)}, f32[128,256]{1,0:T(8,128)}, u32[]{:S(2)}) copy-start(f32[128,256]{1,0:T(8,128)} %w_self.1) | copy-start | bytes 393220
  19.1 3.4 %copy-start.3 = (f32[128,256]{1,0:T(8,128)S(1)}, f32[128,256]{1,0:T(8,128)}, u32[]{:S(2)}) copy-start(f32[128,256]{1,0:T(8,128)} %w_neigh.1) | copy-start | bytes 393220
  19.2 3.4 %copy-start.4 = (f32[256]{0:T(256)S(1)}, f32[256]{0:T(256)}, u32[]{:S(2)}) copy-start(f32[256]{0:T(256)} %param.13) | copy-start | bytes 3076

commit v7 on v6

--- a/solution.py
+++ b/solution.py
@@ -482,11 +482,6 @@
     for off in far_first:
         for axis in (0, 1):
             ag2(axis, 0, off).start()
-    hidden = preact * gating
-    for core in (0, 1):
-        hidden_half[core] = hidden[:, core * hid : (core + 1) * hid]
-    hidden_pair = remote(hidden_half.at[other], hidden_got, pair_send.at[1], pair_recv.at[1], rep=other)
-    hidden_pair.start()
     grad_self = dot3(feat[rep].T, grad_parts)
     grad_neigh = dot3(aggregate.T, grad_parts)
     grad_bias = jnp.sum(grad_pre, axis=0, keepdims=True)
@@ -498,28 +493,33 @@
         grads[core, :, share:] = jnp.broadcast_to(grad_bias[None, :, span], (cols, 8, hid))
     grads_pair = remote(grads.at[other], grads_got, pair_send.at[0], pair_recv.at[0], rep=other)
     grads_pair.start()
+    hidden = preact * gating
+    for core in (0, 1):
+        hidden_half[core] = hidden[:, core * hid : (core + 1) * hid]
+    hidden_pair = remote(hidden_half.at[other], hidden_got, pair_send.at[1], pair_recv.at[1], rep=other)
+    hidden_pair.start()
     for off in (1, 3, 2):
         for axis in (0, 1):
             ag1(axis, off, arrives=True).wait_recv()
             for ahead in far_first:
                 ag2(axis, off, ahead).start()
+    grads_pair.wait_recv()
+    grads[rep] += grads_got[...]
+
+    def to_col(off, arrives=False):
+        return remote(
+            grads.at[rep, (z + off) % cols], grads_col.at[(z + cols - off) % cols if arrives else z],
+            col_send.at[off - 1], col_recv.at[off - 1], col=(z + off) % cols,
+        )
+
+    pl.semaphore_wait(near_in.at[1], 2)
+    for off in around:
+        to_col(off).start()
+    grads_col[z] = grads[rep, z]
     direct = dot3(self_parts, grad_parts, ((1,), (1,)))
     direct_half[...] = direct.reshape(2, width // 2, block)
     direct_pair = remote(direct_half.at[other], direct_got, pair_send.at[2], pair_recv.at[2], rep=other)
     direct_pair.start()
-    grads_pair.wait_recv()
-    grads[rep] += grads_got[...]
-
-    def to_col(off, arrives=False):
-        return remote(
-            grads.at[rep, (z + off) % cols], grads_col.at[(z + cols - off) % cols if arrives else z],
-            col_send.at[off - 1], col_recv.at[off - 1], col=(z + off) % cols,
-        )
-
-    pl.semaphore_wait(near_in.at[1], 2)
-    for off in around:
-        to_col(off).start()
-    grads_col[z] = grads[rep, z]
     hidden_out[rep] = hidden_half[rep]
     direct_out[rep] = direct_half[rep]
     for axis in (0, 1):

time: 69 us -> 69.7 us (1.010)
  Pallas kernels: 66.7 us -> 67.5 us
    pallas_call x1, Pallas kernels: 18.3 us -> 16.5 us  [last(): pl.pallas_call(functools.partial(last_kernel, cols, factor), out_shape=(V...]
    pallas_call x1, Pallas kernels: 3.34 us -> 4.35 us  [forward(): pl.pallas_call(forward_kernel, out_shape=jax.ShapeDtypeStruct(out_shape,...]
    pallas_call x1, Pallas kernels: 2.58 us -> 3.56 us  [backward(): pl.pallas_call(backward_kernel, out_shape=(shape(out_shape, F32), shape(h...]
where the time goes in v7:
time: 69.7 us; the launch traced here: 68.9 us
  Pallas kernels  67.5 us (97%)
  between operations  1.4 us (2%)
    pallas_call x1, Pallas kernels, middle(): pl.pallas_call(middle_kernel, out_shape=(shape((2, block, hid), F32), sha...  24.6 us
    pallas_call x1, Pallas kernels, gather_features(): pl.pallas_call(functools.partial(gather_kernel, cols, (rows, 2 * cols)),...  17.8 us
    pallas_call x1, Pallas kernels, last(): pl.pallas_call(functools.partial(last_kernel, cols, factor), out_shape=(V...  16.5 us
    pallas_call x1, Pallas kernels, forward(): pl.pallas_call(forward_kernel, out_shape=jax.ShapeDtypeStruct(out_shape,...  4.35 us
    pallas_call x1, Pallas kernels, backward(): pl.pallas_call(backward_kernel, out_shape=(shape(out_shape, F32), shape(h...  3.56 us

profile of v7, /device:TPU:1, one launch (start us, length us, event | category | flops | bytes accessed | tf_op | source)
XLA Modules:
  0.0 68.9 jit_solution(11627443522308807539)
XLA Ops:
  1.3 17.8 %gather_features.1 = (bf16[16,256,256]{2,1,0:T(8,128)(2,1)S(1)}, s32[8,256]{1,0:T(8,128)S(1)}, f32[184,128,128]{2,1,0:T(8,128)S(1)}) custom-call(s32[1,1]{1,0:T(1,128)S(6)} %copy.14.count, s32[1,1,184]{2,1,0:T(1,128)} %dst_far.1, s32[1,1,184]{2,1,0:T(1,128)} %src_far.1, f32[2,128,128]{2,1,0:T(8,128)} %bitcast.8, f32[184,128,128]{2,1,0:T(8,128)} %bitcast.13), custom_call_target="tpu_custom_call" | custom-call | tf_op jit(solution)/shard_map/gather_features/pallas_call | solution.py:197
  19.1 0.0 copy-start
  19.1 0.0 copy-start.1
  19.1 0.0 copy-start.2
  19.1 0.0 copy-start.3
  19.2 0.0 copy-start.4
  19.2 4.3 %forward.1.sums = f32[5,4,136,128]{3,2,1,0:T(8,128)S(1)} custom-call(s32[8,256]{1,0:T(8,128)S(1)} %get-tuple-element.21.lists, f32[184,128,128]{2,1,0:T(8,128)S(1)} %get-tuple-element.22.tiles, bf16[16,256,256]{2,1,0:T(8,128)(2,1)S(1)} %get-tuple-element.23.stacked), custom_call_target="tpu_custom_call" | custom-call | tf_op jit(solution)/shard_map/forward/pallas_call | solution.py:294
  23.5 0.0 copy-done
  23.5 0.0 copy-done.1
  23.5 0.0 copy-done.2
  23.6 0.0 copy-done.3
  23.6 0.0 copy-done.4
  23.6 24.6 %middle.1 = (f32[2,128,128]{2,1,0:T(8,128)S(1)}, bf16[16,128,256]{2,1,0:T(8,128)(2,1)S(1)}, f32[2,64,128]{2,1,0:T(8,128)S(1)}, f32[40,128]{1,0:T(8,128)S(1)}) custom-call(f32[5,4,136,128]{3,2,1,0:T(8,128)S(1)} %forward.1.sums, f32[2,128,128]{2,1,0:T(8,128)S(1)} %bitcast.9, f32[2,128,256]{2,1,0:T(8,128)S(1)} %bitcast.10, f32[128,256]{1,0:T(8,128)S(1)} %copy-done.2, ...), custom_call_target="tpu_custom_call" | custom-call | tf_op jit(solution)/shard_map/middle/pallas_call | solution.py:569
  48.2 3.6 %backward.1 = (f32[17,128,128]{2,1,0:T(8,128)S(1)}, f32[2,128,128]{2,1,0:T(8,128)}) custom-call(s32[8,256]{1,0:T(8,128)S(1)} %get-tuple-element.21.lists, f32[184,128,128]{2,1,0:T(8,128)S(1)} %get-tuple-element.22.tiles, bf16[16,128,256]{2,1,0:T(8,128)(2,1)S(1)} %get-tuple-element.24.stacked, f32[2,128,128]{2,1,0:T(8,128)S(1)} %get-tuple-element.25.hidden), custom_call_target="tpu_custom_call" | custom-call | tf_op jit(solution)/shard_map/backward/pallas_call | solution.py:308
  51.8 16.5 %last.1 = (f32[2,64,128]{2,1,0:T(8,128)S(1)}, f32[8,32,128]{2,1,0:T(8,128)S(1)}, f32[8,128]{1,0:T(8,128)S(1)}) custom-call(f32[17,128,128]{2,1,0:T(8,128)S(1)} %get-tuple-element.27.sums, f32[2,64,128]{2,1,0:T(8,128)S(1)} %get-tuple-element.28.direct, f32[40,128]{1,0:T(8,128)S(1)} %get-tuple-element.29.grad_part), custom_call_target="tpu_custom_call" | custom-call | tf_op jit(solution)/shard_map/last/pallas_call | solution.py:753
  68.2 0.7 %finish.1 = (f32[64,256]{1,0:T(8,128)}, f32[128,128]{1,0:T(8,128)}, f32[128,128]{1,0:T(8,128)}, f32[1,128]{1,0:T(1,128)}) custom-call(f32[2,64,128]{2,1,0:T(8,128)S(1)} %get-tuple-element.30.grad_feat, f32[2,128,128]{2,1,0:T(8,128)S(1)} %bitcast.11, f32[8,128]{1,0:T(8,128)S(1)} %get-tuple-element.32.grad_bias), custom_call_target="tpu_custom_call" | custom-call | tf_op jit(solution)/shard_map/finish/pallas_call | solution.py:812
Async XLA Ops:
  19.1 4.4 %copy-start = (f32[256,128]{1,0:T(8,128)S(1)}, f32[256,128]{1,0:T(8,128)}, u32[]{:S(2)}) copy-start(f32[256,128]{1,0:T(8,128)} %param.9) | copy-start | bytes 393220
  19.1 4.4 %copy-start.1 = (f32[256,256]{1,0:T(8,128)S(1)}, f32[256,256]{1,0:T(8,128)}, u32[]{:S(2)}) copy-start(f32[256,256]{1,0:T(8,128)} %param.10) | copy-start | bytes 786436
  19.1 4.4 %copy-start.2 = (f32[128,256]{1,0:T(8,128)S(1)}, f32[128,256]{1,0:T(8,128)}, u32[]{:S(2)}) copy-start(f32[128,256]{1,0:T(8,128)} %w_self.1) | copy-start | bytes 393220
  19.1 4.4 %copy-start.3 = (f32[128,256]{1,0:T(8,128)S(1)}, f32[128,256]{1,0:T(8,128)}, u32[]{:S(2)}) copy-start(f32[128,256]{1,0:T(8,128)} %w_neigh.1) | copy-start | bytes 393220
  19.2 4.4 %copy-start.4 = (f32[256]{0:T(256)S(1)}, f32[256]{0:T(256)}, u32[]{:S(2)}) copy-start(f32[256]{0:T(256)} %param.13) | copy-start | bytes 3076
